TPU v7x, 128 devices: a whole 4x4x4 slice. The times are simulated.
128 devices in a mesh: pipe: 2 (over core), dp: 16 (over y, z), mp: 4 (over x).
Axes of the slice: x: 4, y: 4, z: 4, core: 2. Of those that a mesh axis runs over, the one named last changes fastest.
Arguments:
- states: bfloat16 [2, 32, 512, 512], P('pipe', 'dp', 'mp'), may hold values from -6 to 6
- cotangent: bfloat16 [2, 32, 512, 512], P('pipe', 'dp', 'mp'), may hold values from -6 to 6
- halting: int32 [2, 32, 512], P('pipe', 'dp', 'mp'), may hold values from 0 to 1, as said below
- segments: int32 [2, 32, 512], P(None, 'dp'), may hold values from 0 to 4, as said below
- norm_gain: float32 [2, 3, 512], P('pipe'), may hold values from 0.5 to 1.5
- norm_bias: float32 [2, 3, 512], P('pipe'), may hold values from -1 to 1
- attn_in: bfloat16 [2, 512, 3, 512], P('pipe', 'dp', None, 'mp'), may hold values from -0.25 to 0.25
- attn_out: bfloat16 [2, 512, 512], P('pipe', 'mp', 'dp'), may hold values from -2 to 2
- cross: bfloat16 [2, 512, 2, 512], P('pipe', 'dp', None, 'mp'), may hold values from -6 to 6, as said below
- up_weight: bfloat16 [2, 512, 2048], P('pipe', 'dp', 'mp'), may hold values from -0.25 to 0.25
- up_bias: float32 [2, 2048], P('pipe'), may hold values from -1 to 1
- down_weight: bfloat16 [2, 2048, 512], P('pipe', 'mp', 'dp'), may hold values from -0.125 to 0.125
- down_bias: float32 [2, 512], P('pipe'), may hold values from -1 to 1
- halt_weight: float32 [2, 512], P('pipe'), may hold values from -0.25 to 0.25
- halt_bias: float32 [2], P('pipe'), may hold values from -1 to 1
Outputs:
- states_out: bfloat16 [2, 32, 512, 512], P('pipe', 'dp', 'mp')
- states_grad: float32 [2, 32, 512, 512], P('pipe', 'dp', 'mp')
- norm_gain_grad: float32 [2, 3, 512], P('pipe')
- norm_bias_grad: float32 [2, 3, 512], P('pipe')
- attn_in_grad: float32 [2, 512, 3, 512], P('pipe', 'dp', None, 'mp')
- attn_out_grad: float32 [2, 512, 512], P('pipe', 'mp', 'dp')
- cross_grad: float32 [2, 512, 2, 512], P('pipe', 'dp', None, 'mp')
- up_weight_grad: float32 [2, 512, 2048], P('pipe', 'dp', 'mp')
- up_bias_grad: float32 [2, 2048], P('pipe')
- down_weight_grad: float32 [2, 2048, 512], P('pipe', 'mp', 'dp')
- down_bias_grad: float32 [2, 512], P('pipe')
- halt_weight_grad: float32 [2, 512], P('pipe')
- halt_bias_grad: float32 [2], P('pipe')
- act_stats: float32 [2, 2], P('pipe')
Inputs may be any that keep to these rules, and one draw needn't show every extreme that they name: `halting`: a row's first position is always 1. `segments`: document numbers never fall along a row; each row of either side holds all 5 documents, so a target document always has a source document of the same number in the same row; document 2 starts within the first 128 positions of its row and ends within the last 128. `cross`: independent entries of zero mean.
All inputs are finite; a program needn't handle non-finite values.
Results may differ from a plain program's by a relative error of at most 0.023.
Values may be sent and summed in bfloat16 or wider, within the bound.
A program may use at most 128 MiB of HBM per device.

v0:
```python
import jax
import jax.numpy as jnp
from jax import lax
from jax.sharding import PartitionSpec as P

HEAD_DIM = 64


EPS = 1e-06


def passed_along(value, axis, steps):
    count = lax.axis_size(axis)
    leading, last = (max(0, -steps), min(count, count - steps))
    return lax.ppermute(value, axis, [(source, source + steps) for source in range(leading, last)])


def normalize(value, gain, shift):
    center = value - jnp.mean(value, axis=-1, keepdims=True)
    spread = jnp.mean(center * center, axis=-1, keepdims=True)
    factor = lax.rsqrt(spread + EPS)
    unit = center * factor
    return (unit * gain + shift, (unit, factor))


def norm_back(grad, saved, gain):
    unit, factor = saved
    scaled = grad * gain
    mean_plain = jnp.mean(scaled, axis=-1, keepdims=True)
    mean_unit = jnp.mean(scaled * unit, axis=-1, keepdims=True)
    return (
        factor * (scaled - mean_plain - unit * mean_unit),
        jnp.sum(grad * unit, 0),
        jnp.sum(grad, 0),
    )


def allowed_block(seg_block, key_seg, offset, causal):
    q_place = offset + jnp.arange(seg_block.shape[0], dtype=jnp.int32)
    k_place = jnp.arange(key_seg.shape[0], dtype=jnp.int32)
    same = seg_block[:, None] == key_seg[None, :]
    order = jnp.logical_or(q_place[:, None] >= k_place[None, :], jnp.logical_not(causal))
    return jnp.logical_and(same, order)


def score_block(q_block, key_rows, allowed, scale):
    scores = (
        jnp.einsum("qhd,khd->hqk", q_block, key_rows, preferred_element_type=jnp.float32) * scale
    )
    return jnp.where(allowed[None], scores, -1e30)


def split_blocks(queries, q_seg):
    length = queries.shape[0]
    rows_block = min(512, length)
    count = length // rows_block
    return (
        queries.reshape(count, rows_block, queries.shape[1], queries.shape[2]),
        q_seg.reshape(count, rows_block),
        jnp.arange(count, dtype=jnp.int32) * rows_block,
    )


def attend_fwd(queries, key_rows, values, q_seg, key_seg, causal):
    scale = queries.shape[2] ** (-0.5)

    def one_block(entry):
        q_block, seg_block, offset = entry
        scores = score_block(
            q_block, key_rows, allowed_block(seg_block, key_seg, offset, causal), scale
        )
        highest = jnp.max(scores, axis=-1, keepdims=True)
        powers = jnp.exp(scores - highest)
        totals = jnp.sum(powers, axis=-1, keepdims=True)
        probs = powers / totals
        result = jnp.einsum(
            "hqk,khd->qhd", probs.astype(jnp.bfloat16), values, preferred_element_type=jnp.float32
        )
        return (result.astype(jnp.bfloat16), (highest + jnp.log(totals))[..., 0])

    outs, logsum = lax.map(one_block, split_blocks(queries, q_seg))
    return (outs.reshape(queries.shape), logsum)


def attend_back(queries, key_rows, values, q_seg, key_seg, causal, logsum, grad_out):
    scale = queries.shape[2] ** (-0.5)
    q_blocks, seg_blocks, offsets = split_blocks(queries, q_seg)
    g_blocks = grad_out.reshape(q_blocks.shape)

    def one_block(carry, entry):
        key_acc, value_acc = carry
        q_block, seg_block, offset, lse_block, g_block = entry
        scores = score_block(
            q_block, key_rows, allowed_block(seg_block, key_seg, offset, causal), scale
        )
        probs = jnp.exp(scores - lse_block[..., None])
        d_probs = jnp.einsum("qhd,khd->hqk", g_block, values, preferred_element_type=jnp.float32)
        delta = jnp.sum(probs * d_probs, axis=-1, keepdims=True)
        d_scores = (probs * (d_probs - delta) * scale).astype(jnp.bfloat16)
        d_query = jnp.einsum("hqk,khd->qhd", d_scores, key_rows, preferred_element_type=jnp.float32)
        key_acc = key_acc + jnp.einsum(
            "hqk,qhd->khd", d_scores, q_block, preferred_element_type=jnp.float32
        )
        value_acc = value_acc + jnp.einsum(
            "hqk,qhd->khd", probs.astype(jnp.bfloat16), g_block, preferred_element_type=jnp.float32
        )
        return ((key_acc, value_acc), d_query.astype(jnp.bfloat16))

    start = (jnp.zeros(key_rows.shape, jnp.float32), jnp.zeros(values.shape, jnp.float32))
    (key_acc, value_acc), d_query = lax.scan(
        one_block, start, (q_blocks, seg_blocks, offsets, logsum, g_blocks)
    )
    return (
        d_query.reshape(queries.shape),
        key_acc.astype(jnp.bfloat16),
        value_acc.astype(jnp.bfloat16),
    )


def place(buffer, value, micro, valid):
    current = lax.dynamic_index_in_dim(buffer, micro, 0, keepdims=False)
    return lax.dynamic_update_index_in_dim(buffer, jnp.where(valid, value, current), micro, 0)


def on_device(
    states,
    cotangent,
    halting,
    segments,
    norm_gain,
    norm_bias,
    attn_in,
    attn_out,
    cross,
    up_weight,
    up_bias,
    down_weight,
    down_bias,
    halt_weight,
    halt_bias,
):
    section = lax.axis_index("pipe")
    encoding = section == 0
    decoding = jnp.logical_not(encoding)
    model_index = lax.axis_index("mp")
    micro_count = states.shape[1]
    tokens_here = states.shape[2]
    width = states.shape[3]
    length = tokens_here * lax.axis_size("mp")
    hidden_here = up_weight.shape[2]
    hidden_all = up_bias.shape[1]
    head_width = attn_in.shape[3]
    local_heads = head_width // HEAD_DIM
    rows_block = min(512, length)
    block_count = length // rows_block
    gains = norm_gain[0]
    shifts = norm_bias[0]
    up_shift = lax.dynamic_slice_in_dim(up_bias[0], model_index * hidden_here, hidden_here)
    down_shift = down_bias[0]
    halt_vector = halt_weight[0]
    halt_shift = halt_bias[0]

    def collect():
        return (
            lax.all_gather(attn_in[0], "dp", axis=0, tiled=True),
            lax.all_gather(attn_out[0], "dp", axis=1, tiled=True),
            lax.all_gather(cross[0], "dp", axis=0, tiled=True),
            lax.all_gather(up_weight[0], "dp", axis=0, tiled=True),
            lax.all_gather(down_weight[0], "dp", axis=1, tiled=True),
        )

    def spread(g_in, g_out, g_cross, g_up, g_down):
        return (
            lax.psum_scatter(
                g_in.astype(jnp.bfloat16), "dp", scatter_dimension=0, tiled=True
            ).astype(jnp.float32),
            lax.psum_scatter(
                g_out.astype(jnp.bfloat16), "dp", scatter_dimension=1, tiled=True
            ).astype(jnp.float32),
            lax.psum_scatter(
                g_cross.astype(jnp.bfloat16), "dp", scatter_dimension=0, tiled=True
            ).astype(jnp.float32),
            lax.psum_scatter(
                g_up.astype(jnp.bfloat16), "dp", scatter_dimension=0, tiled=True
            ).astype(jnp.float32),
            lax.psum_scatter(
                g_down.astype(jnp.bfloat16), "dp", scatter_dimension=1, tiled=True
            ).astype(jnp.float32),
        )

    def rows_in(value):
        return lax.all_gather(value, "mp", axis=0, tiled=True)

    def sums_in(value):
        return lax.psum_scatter(
            value.astype(jnp.bfloat16), "mp", scatter_dimension=0, tiled=True
        ).astype(jnp.float32)

    def rows_back(value):
        return lax.all_gather(value, "mp", axis=0, tiled=True)

    def sums_back(value):
        return lax.psum_scatter(
            value.astype(jnp.bfloat16), "mp", scatter_dimension=0, tiled=True
        ).astype(jnp.float32)

    kept_list = []
    outputs = jnp.zeros((micro_count, tokens_here, width), jnp.bfloat16)
    memory_prev = jnp.zeros((tokens_here, width), jnp.bfloat16)
    stats_global = jnp.zeros((2,), jnp.float32)
    stats_local = jnp.zeros((2,), jnp.float32)
    for tick in range(micro_count + 1):
        weights = collect()
        w_in, w_out, w_cross, w_up, w_down = weights
        micro = jnp.clip(tick - section, 0, micro_count - 1)
        valid = jnp.logical_and(tick - section >= 0, tick - section < micro_count)
        inputs = lax.dynamic_index_in_dim(states[0], micro, 0, keepdims=False).astype(jnp.float32)
        running_mask = lax.dynamic_index_in_dim(halting[0], micro, 0, keepdims=False).astype(
            jnp.float32
        )
        seg_src = lax.dynamic_index_in_dim(segments[0], micro, 0, keepdims=False)
        seg_tgt = lax.dynamic_index_in_dim(segments[1], micro, 0, keepdims=False)
        seg_self = jnp.where(encoding, seg_src, seg_tgt)
        normed_one, saved_one = normalize(inputs, gains[0], shifts[0])
        full_one = rows_in(normed_one.astype(jnp.bfloat16))
        triple = jnp.einsum(
            "td,dsh->tsh", full_one, w_in, preferred_element_type=jnp.float32
        ).astype(jnp.bfloat16)
        split = triple.reshape(length, 3, local_heads, HEAD_DIM)
        heads_one, logsum_one = attend_fwd(
            split[:, 0], split[:, 1], split[:, 2], seg_self, seg_self, decoding
        )
        flat_one = heads_one.reshape(length, head_width)
        after_self = inputs + sums_in(jnp.dot(flat_one, w_out, preferred_element_type=jnp.float32))
        normed_two, saved_two = normalize(after_self, gains[1], shifts[1])
        full_two = rows_in(jnp.where(encoding, memory_prev, normed_two.astype(jnp.bfloat16)))

        def enc_proj():
            return jnp.einsum(
                "td,dsh->tsh", full_two, w_cross, preferred_element_type=jnp.float32
            ).astype(jnp.bfloat16)

        def dec_proj():
            asked = jnp.dot(full_two, w_cross[:, 0], preferred_element_type=jnp.float32).astype(
                jnp.bfloat16
            )
            return jnp.stack([asked, jnp.zeros_like(asked)], axis=1)

        projected = lax.cond(encoding, enc_proj, dec_proj)
        pairs_in = passed_along(projected, "pipe", 1)

        def dec_cross():
            asked = projected[:, 0].reshape(length, local_heads, HEAD_DIM)
            pair_heads = pairs_in.reshape(length, 2, local_heads, HEAD_DIM)
            heads_two, logsum_two = attend_fwd(
                asked, pair_heads[:, 0], pair_heads[:, 1], seg_tgt, seg_src, False
            )
            partial_value = jnp.einsum(
                "th,dh->td",
                heads_two.reshape(length, head_width),
                w_cross[:, 1],
                preferred_element_type=jnp.float32,
            )
            return (partial_value, heads_two, logsum_two)

        def enc_cross():
            return (
                jnp.zeros((length, width), jnp.float32),
                jnp.zeros((length, local_heads, HEAD_DIM), jnp.bfloat16),
                jnp.zeros((block_count, local_heads, rows_block), jnp.float32),
            )

        partial_two, heads_two, logsum_two = lax.cond(encoding, enc_cross, dec_cross)
        after_cross = after_self + sums_in(partial_two)
        normed_three, saved_three = normalize(after_cross, gains[2], shifts[2])
        full_three = rows_in(normed_three.astype(jnp.bfloat16))
        pre_act = jnp.dot(full_three, w_up, preferred_element_type=jnp.float32) + up_shift
        activated = jax.nn.gelu(pre_act).astype(jnp.bfloat16)
        after_ffn = (
            after_cross
            + sums_in(jnp.dot(activated, w_down, preferred_element_type=jnp.float32))
            + down_shift
        )
        logit = jnp.dot(inputs, halt_vector, precision=lax.Precision.HIGHEST) + halt_shift
        prob = jax.nn.sigmoid(logit)
        running = running_mask * prob
        stepped = inputs + running[:, None] * (after_ffn - inputs)
        memory, saved_memory = normalize(stepped, gains[1], shifts[1])
        result = jnp.where(encoding, memory, stepped).astype(jnp.bfloat16)
        validf = valid.astype(jnp.float32)
        counts = jnp.stack([jnp.sum(running), jnp.sum(running_mask)]) * validf
        forward_saved = {
            "micro": micro,
            "valid": valid,
            "inputs": inputs,
            "running_mask": running_mask,
            "prob": prob,
            "after_ffn": after_ffn,
            "seg_src": seg_src,
            "seg_tgt": seg_tgt,
            "seg_self": seg_self,
            "saved_one": saved_one,
            "full_one": full_one,
            "triple": triple,
            "flat_one": flat_one,
            "logsum_one": logsum_one,
            "saved_two": saved_two,
            "full_two": full_two,
            "projected": projected,
            "pairs_in": pairs_in,
            "heads_two": heads_two,
            "logsum_two": logsum_two,
            "saved_three": saved_three,
            "full_three": full_three,
            "pre_act": pre_act,
            "activated": activated,
            "saved_memory": saved_memory,
        }
        saved, result, memory_prev, counts = (
            forward_saved,
            result,
            memory.astype(jnp.bfloat16),
            counts,
        )
        outputs = place(outputs, result, saved["micro"], saved["valid"])
        stats_global = stats_global + lax.psum(counts, ("dp", "mp"))
        kept_list.append(saved)
    input_grads = jnp.zeros((micro_count, tokens_here, width), jnp.float32)
    memory_grad = jnp.zeros((tokens_here, width), jnp.float32)
    shard_sum = None
    small_sum = None
    for tick in range(micro_count + 1):
        weights = collect()
        saved = kept_list[micro_count - tick]
        backward_w_in, backward_w_out, backward_w_cross, backward_w_up, backward_w_down = weights
        cross_ok = 1.0 if micro_count - tick >= 1 else 0.0
        backward_micro = saved["micro"]
        backward_validf = saved["valid"].astype(jnp.float32)
        enc_valid = encoding.astype(jnp.float32) * backward_validf
        dec_valid = decoding.astype(jnp.float32) * backward_validf
        backward_inputs = saved["inputs"]
        backward_prob = saved["prob"]
        backward_running_mask = saved["running_mask"]
        incoming = lax.dynamic_index_in_dim(cotangent[0], backward_micro, 0, keepdims=False).astype(
            jnp.float32
        )
        incoming = incoming + jnp.where(encoding, memory_grad, 0.0)
        d_mem_in, gain_mem, shift_mem = norm_back(incoming, saved["saved_memory"], gains[1])
        d_stepped = jnp.where(encoding, d_mem_in, incoming)
        backward_running = backward_running_mask * backward_prob
        d_after_ffn = d_stepped * backward_running[:, None]
        d_inputs = d_stepped * (1.0 - backward_running[:, None])
        d_logit = (
            backward_running_mask
            * jnp.sum(d_stepped * (saved["after_ffn"] - backward_inputs), axis=-1)
            * backward_prob
            * (1.0 - backward_prob)
        )
        d_inputs = d_inputs + d_logit[:, None] * halt_vector[None, :]
        g_halt_vec = jnp.dot(d_logit, backward_inputs, precision=lax.Precision.HIGHEST)
        g_halt_bias = jnp.sum(d_logit)
        g_down_bias = jnp.sum(d_after_ffn, 0)
        d_full_three = rows_back(d_after_ffn.astype(jnp.bfloat16))
        d_activated = jnp.einsum(
            "td,fd->tf", d_full_three, backward_w_down, preferred_element_type=jnp.float32
        )
        d_pre = jax.vjp(jax.nn.gelu, saved["pre_act"])[1](d_activated)[0]
        g_up_bias = jnp.sum(d_pre, 0)
        d_pre_low = d_pre.astype(jnp.bfloat16)
        backward_g_down = jnp.einsum(
            "tf,td->fd", saved["activated"], d_full_three, preferred_element_type=jnp.float32
        )
        backward_g_up = jnp.einsum(
            "td,tf->df", saved["full_three"], d_pre_low, preferred_element_type=jnp.float32
        )
        d_normed_three = sums_back(
            jnp.einsum("tf,df->td", d_pre_low, backward_w_up, preferred_element_type=jnp.float32)
        )
        back_three, gain_three, shift_three = norm_back(
            d_normed_three, saved["saved_three"], gains[2]
        )
        d_after_cross = d_after_ffn + back_three
        d_full_two = rows_back(d_after_cross.astype(jnp.bfloat16))
        backward_projected = saved["projected"]
        backward_heads_two = saved["heads_two"]

        def dec_back():
            d_heads = jnp.einsum(
                "td,dh->th", d_full_two, backward_w_cross[:, 1], preferred_element_type=jnp.float32
            )
            d_heads = d_heads.astype(jnp.bfloat16).reshape(length, local_heads, HEAD_DIM)
            g_out_t = jnp.einsum(
                "td,th->dh",
                d_full_two,
                backward_heads_two.reshape(length, head_width),
                preferred_element_type=jnp.float32,
            )
            asked = backward_projected[:, 0].reshape(length, local_heads, HEAD_DIM)
            pair_heads = saved["pairs_in"].reshape(length, 2, local_heads, HEAD_DIM)
            d_asked, d_keys, d_values = attend_back(
                asked,
                pair_heads[:, 0],
                pair_heads[:, 1],
                saved["seg_tgt"],
                saved["seg_src"],
                False,
                saved["logsum_two"],
                d_heads,
            )
            d_asked = d_asked.reshape(length, head_width)
            own = jnp.stack([d_asked, jnp.zeros_like(d_asked)], axis=1)
            sent = jnp.stack(
                [d_keys.reshape(length, head_width), d_values.reshape(length, head_width)], axis=1
            )
            return (own, sent, g_out_t)

        def enc_back():
            blank = jnp.zeros((length, 2, head_width), jnp.bfloat16)
            return (blank, blank, jnp.zeros((width, head_width), jnp.float32))

        own, sent, g_out_t = lax.cond(encoding, enc_back, dec_back)
        received = passed_along(sent, "pipe", -1)
        d_projected = jnp.where(encoding, received, own)
        backward_g_cross = jnp.einsum(
            "td,tsh->dsh", saved["full_two"], d_projected, preferred_element_type=jnp.float32
        )
        backward_g_cross = backward_g_cross.at[:, 1].add(g_out_t) * cross_ok
        d_gathered = sums_back(
            jnp.einsum(
                "tsh,dsh->td", d_projected, backward_w_cross, preferred_element_type=jnp.float32
            )
        )
        back_two, gain_two, shift_two = norm_back(d_gathered, saved["saved_two"], gains[1])
        memory_next = jnp.where(encoding, d_gathered, 0.0) * cross_ok
        d_after_self = d_after_cross + jnp.where(encoding, 0.0, back_two)
        d_full_one = rows_back(d_after_self.astype(jnp.bfloat16))
        d_heads_one = jnp.einsum(
            "td,hd->th", d_full_one, backward_w_out, preferred_element_type=jnp.float32
        )
        d_heads_one = d_heads_one.astype(jnp.bfloat16).reshape(length, local_heads, HEAD_DIM)
        backward_g_out = jnp.einsum(
            "th,td->hd", saved["flat_one"], d_full_one, preferred_element_type=jnp.float32
        )
        backward_split = saved["triple"].reshape(length, 3, local_heads, HEAD_DIM)
        d_asked, d_keys, d_values = attend_back(
            backward_split[:, 0],
            backward_split[:, 1],
            backward_split[:, 2],
            saved["seg_self"],
            saved["seg_self"],
            decoding,
            saved["logsum_one"],
            d_heads_one,
        )
        d_triple = jnp.stack(
            [
                d_asked.reshape(length, head_width),
                d_keys.reshape(length, head_width),
                d_values.reshape(length, head_width),
            ],
            axis=1,
        )
        backward_g_in = jnp.einsum(
            "td,tsh->dsh", saved["full_one"], d_triple, preferred_element_type=jnp.float32
        )
        d_normed_one = sums_back(
            jnp.einsum("tsh,dsh->td", d_triple, backward_w_in, preferred_element_type=jnp.float32)
        )
        back_one, gain_one, shift_one = norm_back(d_normed_one, saved["saved_one"], gains[0])
        d_inputs = d_inputs + d_after_self + back_one
        tick_grads = (
            backward_g_in * backward_validf,
            backward_g_out * backward_validf,
            backward_g_cross,
            backward_g_up * backward_validf,
            backward_g_down * backward_validf,
        )
        gain_mid = gain_mem * enc_valid + gain_two * dec_valid
        shift_mid = shift_mem * enc_valid + shift_two * dec_valid
        small = (
            jnp.stack([gain_one * backward_validf, gain_mid, gain_three * backward_validf]),
            jnp.stack([shift_one * backward_validf, shift_mid, shift_three * backward_validf]),
            lax.dynamic_update_slice_in_dim(
                jnp.zeros((hidden_all,), jnp.float32),
                g_up_bias * backward_validf,
                model_index * hidden_here,
                0,
            ),
            g_down_bias * backward_validf,
            g_halt_vec * backward_validf,
            g_halt_bias * backward_validf,
        )
        tick_grads, small, d_inputs, memory_grad = (tick_grads, small, d_inputs, memory_next)
        input_grads = place(input_grads, d_inputs, saved["micro"], saved["valid"])
        small_sum = small if small_sum is None else tuple((a + b for a, b in zip(small_sum, small)))
        pieces = spread(*tick_grads)
        shard_sum = (
            pieces if shard_sum is None else tuple((a + b for a, b in zip(shard_sum, pieces)))
        )
    totals = lax.psum(
        (
            small_sum[0],
            small_sum[1],
            small_sum[2],
            small_sum[3],
            small_sum[4],
            small_sum[5],
            stats_local,
        ),
        ("dp", "mp"),
    )
    stats = stats_global + totals[6]
    all_tokens = micro_count * tokens_here * lax.axis_size("dp") * lax.axis_size("mp")
    act_stats = jnp.stack([stats[0] / stats[1], 1.0 - stats[1] / all_tokens])[None]
    return (
        outputs[None],
        input_grads[None],
        totals[0][None],
        totals[1][None],
        shard_sum[0][None],
        shard_sum[1][None],
        shard_sum[2][None],
        shard_sum[3][None],
        totals[2][None],
        shard_sum[4][None],
        totals[3][None],
        totals[4][None],
        jnp.reshape(totals[5], (1,)),
        act_stats,
    )


def solution(mesh):
    return jax.shard_map(
        on_device,
        mesh=mesh,
        in_specs=(
            P("pipe", "dp", "mp", None),
            P("pipe", "dp", "mp", None),
            P("pipe", "dp", "mp"),
            P(None, "dp", None),
            P("pipe", None, None),
            P("pipe", None, None),
            P("pipe", "dp", None, "mp"),
            P("pipe", "mp", "dp"),
            P("pipe", "dp", None, "mp"),
            P("pipe", "dp", "mp"),
            P("pipe", None),
            P("pipe", "mp", "dp"),
            P("pipe", None),
            P("pipe", None),
            P("pipe"),
        ),
        out_specs=(
            P("pipe", "dp", "mp", None),
            P("pipe", "dp", "mp", None),
            P("pipe", None, None),
            P("pipe", None, None),
            P("pipe", "dp", None, "mp"),
            P("pipe", "mp", "dp"),
            P("pipe", "dp", None, "mp"),
            P("pipe", "dp", "mp"),
            P("pipe", None),
            P("pipe", "mp", "dp"),
            P("pipe", None),
            P("pipe", None),
            P("pipe"),
            P("pipe", None),
        ),
        check_vma=False,
    )
```

profile of v0, /device:TPU:0, one launch (start us, length us, event | category | flops | bytes accessed | tf_op | source)
XLA Modules:
  0.0 2300.0 jit_solution(12333150417816879541)
XLA Ops:
  11.8 25.2 %all-gather.1 = bf16[1,128,512]{1,2,0:T(8,128)(2,1)S(1)} all-gather(bf16[1,128,32]{1,2,0:T(8,128)(2,1)} %param.46), channel_id=3, replica_groups=mesh['pipe'=2,'dp'=16,'mp'=4] {'dp'}, dimensions={2}, use_global_device_ids=true | all-gather | bytes 139264 | tf_op jit(solution)/shard_map/all_gather | solution.py:166
  37.0 23.3 %all-gather = bf16[1,512,3,128]{3,1,2,0:T(8,128)(2,1)S(1)} all-gather(bf16[1,32,3,128]{3,1,2,0:T(8,128)(2,1)} %param.45), channel_id=2, replica_groups=mesh['pipe'=2,'dp'=16,'mp'=4] {'dp'}, dimensions={1}, use_global_device_ids=true | all-gather | bytes 417792 | tf_op jit(solution)/shard_map/all_gather | solution.py:165
  61.5 13.1 all_gather.105
  80.0 19.1 reduce-scatter.52.cloned.1.call-done
  100.4 12.8 all_gather.46
  113.2 13.2 all_gather.102
  134.4 23.9 %all-gather.2 = bf16[1,512,2,128]{3,1,2,0:T(8,128)(2,1)S(1)} all-gather(bf16[1,32,2,128]{3,1,2,0:T(8,128)(2,1)S(1)} %copy.183), channel_id=4, replica_groups=mesh['pipe'=2,'dp'=16,'mp'=4] {'dp'}, dimensions={1}, use_global_device_ids=true | all-gather | bytes 278528 | tf_op jit(solution)/shard_map/all_gather | solution.py:167
  158.3 18.2 reduce-scatter.46.cloned.1.call-done
  180.0 12.8 all_gather.98
  198.8 24.5 %all-gather.3 = bf16[1,512,512]{2,1,0:T(8,128)(2,1)S(1)} all-gather(bf16[1,32,512]{2,1,0:T(8,128)(2,1)S(1)} %copy-done.135), channel_id=5, replica_groups=mesh['pipe'=2,'dp'=16,'mp'=4] {'dp'}, dimensions={1}, use_global_device_ids=true | all-gather | bytes 557056 | tf_op jit(solution)/shard_map/all_gather | solution.py:168
  223.2 25.2 %all-gather.4 = bf16[1,512,512]{1,2,0:T(8,128)(2,1)} all-gather(bf16[1,512,32]{1,2,0:T(8,128)(2,1)S(1)} %copy-done.136), channel_id=6, replica_groups=mesh['pipe'=2,'dp'=16,'mp'=4] {'dp'}, dimensions={2}, use_global_device_ids=true | all-gather | bytes 557056 | tf_op jit(solution)/shard_map/all_gather | solution.py:169
  250.0 13.2 all_gather.99
  268.7 15.6 reduce-scatter.44.cloned.1.call-done
  285.8 12.8 all_gather.103
  304.3 28.2 %reduce-scatter.48.cloned.1.call-done = bf16[128,512]{1,0:T(8,128)(2,1)} async-done(((bf16[512,512]{1,0:T(8,128)(2,1)}), bf16[128,512]{1,0:T(8,128)(2,1)}) %reduce-scatter.48.cloned.1.call-update) | async-done | bytes 131088 | tf_op jit(solution)/shard_map/reduce_scatter | solution.py:195
  333.8 12.8 all_gather.104
  351.3 21.2 reduce-scatter.50.cloned.1.call-done
  374.1 13.5 all_gather.106
  395.8 29.2 %reduce-scatter.54.cloned.1.call-done = bf16[128,512]{1,0:T(8,128)(2,1)} async-done(((bf16[512,512]{1,0:T(8,128)(2,1)}), bf16[128,512]{1,0:T(8,128)(2,1)}) %reduce-scatter.54.cloned.1.call-update) | async-done | bytes 131088 | tf_op jit(solution)/shard_map/reduce_scatter | solution.py:195
  427.0 12.8 all_gather.107
  443.5 21.2 reduce-scatter.56.cloned.1.call-done
  469.6 12.8 all_gather.108
  486.1 21.2 reduce-scatter.58.cloned.1.call-done
  510.9 12.8 all_gather.109
  526.6 21.6 collective-permute-done.3
  550.1 22.0 reduce-scatter.60.cloned.1.call-done
  575.9 12.8 all_gather.111
  592.6 21.1 reduce-scatter.64.cloned.1.call-done
  617.3 12.8 all_gather.112
  633.0 20.7 collective-permute-done.4
  655.6 21.9 reduce-scatter.66.cloned.1.call-done
  682.5 12.8 all_gather.114
  705.0 15.3 reduce-scatter.70.cloned.1.call-done
  723.8 12.8 all_gather.115
  738.2 16.1 collective-permute-done.5
  767.9 4.5 fusion.460
  783.7 11.9 reduce-scatter.100.cloned.1.call-done
  803.9 66.7 %reduce-scatter.102.cloned.1.call-done = bf16[32,512]{1,0:T(8,128)(2,1)} async-done(((bf16[512,512]{1,0:T(8,128)(2,1)}), bf16[32,512]{1,0:T(8,128)(2,1)}) %reduce-scatter.102.cloned.1.call-update) | async-done | bytes 32784
  878.2 15.9 reduce-scatter.72.cloned.1.call-done
  897.2 12.8 all_gather.110
  911.0 13.3 all_gather.113
  929.3 13.2 all_gather.116
  950.0 5.3 fusion.168
  957.4 5.3 fusion.171
  964.8 4.2 fusion.174
  976.3 4.2 fusion.177
  991.4 3.4 fusion.183
  994.9 3.5 fusion.180
  1005.4 39.2 %reduce-scatter.94.cloned.1.call-done = bf16[32,512]{1,0:T(8,128)(2,1)} async-done(((bf16[512,512]{1,0:T(8,128)(2,1)}), bf16[32,512]{1,0:T(8,128)(2,1)}) %reduce-scatter.94.cloned.1.call-update) | async-done | bytes 32784 | tf_op jit(solution)/shard_map/reduce_scatter | solution.py:183
  1044.6 74.7 %reduce-scatter.96.cloned.1.call-done = bf16[32,512]{1,0:T(8,128)(2,1)} async-done(((bf16[512,512]{1,0:T(8,128)(2,1)}), bf16[32,512]{1,0:T(8,128)(2,1)}) %reduce-scatter.96.cloned.1.call-update) | async-done | bytes 32784 | tf_op jit(solution)/shard_map/reduce_scatter | solution.py:183
  1119.2 75.2 %reduce-scatter.98.cloned.1.call-done = bf16[32,512]{1,0:T(8,128)(2,1)} async-done(((bf16[512,512]{1,0:T(8,128)(2,1)}), bf16[32,512]{1,0:T(8,128)(2,1)}) %reduce-scatter.98.cloned.1.call-update) | async-done | bytes 32784 | tf_op jit(solution)/shard_map/reduce_scatter | solution.py:183
  1197.7 71.4 %reduce-scatter.88.cloned.1.call-done = bf16[32,2,128]{2,0,1:T(8,128)(2,1)} async-done(((bf16[512,2,128]{2,0,1:T(8,128)(2,1)}), bf16[32,2,128]{2,0,1:T(8,128)(2,1)}) %reduce-scatter.88.cloned.1.call-update) | async-done | bytes 16400 | tf_op jit(solution)/shard_map/reduce_scatter | solution.py:180
  1269.0 75.0 %reduce-scatter.90.cloned.1.call-done = bf16[32,2,128]{2,0,1:T(8,128)(2,1)} async-done(((bf16[512,2,128]{2,0,1:T(8,128)(2,1)}), bf16[32,2,128]{2,0,1:T(8,128)(2,1)}) %reduce-scatter.90.cloned.1.call-update) | async-done | bytes 16400 | tf_op jit(solution)/shard_map/reduce_scatter | solution.py:180
  1344.0 74.5 %reduce-scatter.92.cloned.1.call-done = bf16[32,2,128]{2,0,1:T(8,128)(2,1)} async-done(((bf16[512,2,128]{2,0,1:T(8,128)(2,1)}), bf16[32,2,128]{2,0,1:T(8,128)(2,1)}) %reduce-scatter.92.cloned.1.call-update) | async-done | bytes 16400 | tf_op jit(solution)/shard_map/reduce_scatter | solution.py:180
  1421.3 71.9 %reduce-scatter.82.cloned.1.call-done = bf16[128,32]{0,1:T(8,128)(2,1)} async-done(((bf16[128,512]{0,1:T(8,128)(2,1)}), bf16[128,32]{0,1:T(8,128)(2,1)}) %reduce-scatter.82.cloned.1.call-update) | async-done | bytes 8208 | tf_op jit(solution)/shard_map/reduce_scatter | solution.py:177
  1493.2 74.3 %reduce-scatter.84.cloned.1.call-done = bf16[128,32]{0,1:T(8,128)(2,1)} async-done(((bf16[128,512]{0,1:T(8,128)(2,1)}), bf16[128,32]{0,1:T(8,128)(2,1)}) %reduce-scatter.84.cloned.1.call-update) | async-done | bytes 8208 | tf_op jit(solution)/shard_map/reduce_scatter | solution.py:177
  1567.6 74.7 %reduce-scatter.86.cloned.1.call-done = bf16[128,32]{0,1:T(8,128)(2,1)} async-done(((bf16[128,512]{0,1:T(8,128)(2,1)}), bf16[128,32]{0,1:T(8,128)(2,1)}) %reduce-scatter.86.cloned.1.call-update) | async-done | bytes 8208 | tf_op jit(solution)/shard_map/reduce_scatter | solution.py:177
  1643.6 73.4 %reduce-scatter.80.cloned.1.call-done = bf16[32,3,128]{2,0,1:T(8,128)(2,1)} async-done(((bf16[512,3,128]{2,0,1:T(8,128)(2,1)}), bf16[32,3,128]{2,0,1:T(8,128)(2,1)}) %reduce-scatter.80.cloned.1.call-update) | async-done | bytes 24592 | tf_op jit(solution)/shard_map/reduce_scatter | solution.py:174
  1717.0 75.2 %reduce-scatter.78.cloned.1.call-done = bf16[32,3,128]{2,0,1:T(8,128)(2,1)} async-done(((bf16[512,3,128]{2,0,1:T(8,128)(2,1)}), bf16[32,3,128]{2,0,1:T(8,128)(2,1)}) %reduce-scatter.78.cloned.1.call-update) | async-done | bytes 24592 | tf_op jit(solution)/shard_map/reduce_scatter | solution.py:174
  1792.2 74.6 %reduce-scatter.76.cloned.1.call-done = bf16[32,3,128]{2,0,1:T(8,128)(2,1)} async-done(((bf16[512,3,128]{2,0,1:T(8,128)(2,1)}), bf16[32,3,128]{2,0,1:T(8,128)(2,1)}) %reduce-scatter.76.cloned.1.call-update) | async-done | bytes 24592 | tf_op jit(solution)/shard_map/reduce_scatter | solution.py:174
  1868.2 21.8 reduce-scatter.74.cloned.1.call-done
  1890.0 23.7 %reduce-scatter.68.cloned.1.call-done = bf16[128,512]{1,0:T(8,128)(2,1)} async-done(((bf16[512,512]{1,0:T(8,128)(2,1)}), bf16[128,512]{1,0:T(8,128)(2,1)}) %reduce-scatter.68.cloned.1.call-update) | async-done | bytes 131088 | tf_op jit(solution)/shard_map/reduce_scatter | solution.py:203
  1913.7 24.1 %reduce-scatter.62.cloned.1.call-done = bf16[128,512]{1,0:T(8,128)(2,1)} async-done(((bf16[512,512]{1,0:T(8,128)(2,1)}), bf16[128,512]{1,0:T(8,128)(2,1)}) %reduce-scatter.62.cloned.1.call-update) | async-done | bytes 131088 | tf_op jit(solution)/shard_map/reduce_scatter | solution.py:203
  1939.6 347.2 %all-reduce.6 = (f32[1,3,512]{2,0,1:T(1,128)}, f32[1,3,512]{2,0,1:T(1,128)}, f32[1,2048]{1,0:T(1,128)}, f32[1,512]{1,0:T(1,128)}, f32[1,512]{1,0:T(1,128)}, /*index=5*/f32[1]{0:T(128)}, f32[2]{0:T(128)S(1)}) all-reduce(f32[1,3,512]{2,0,1:T(1,128)S(1)} %broadcast_in_dim.474, ...), channel_id=1, replica_groups=mesh['pipe'=2,'dp'=16,'mp'=4] {'dp','mp'}, use_global_device_ids=true, to_apply=%region_117.118 | all-reduce | flops 6147 | bytes 49176 | tf_op jit(solution)/shard_map/psum | solution.py:500
  (839 shorter events, 223.6 us)
Async XLA Ops:
  7.2 91.9 %reduce-scatter.52.cloned.1.call-start = ((), (), s32[]{:S(2)}) async-start(), calls=%async_computation.39 | async-start | bytes 655360 | tf_op jit(solution)/shard_map/reduce_scatter | solution.py:195
  79.6 78.7 %reduce-scatter.40.cloned.1.call-start = ((), (), s32[]{:S(2)}) async-start(), calls=%async_computation.33 | async-start | bytes 655360 | tf_op jit(solution)/shard_map/reduce_scatter | solution.py:195
  131.1 45.4 %reduce-scatter.46.cloned.1.call-start = ((), (), s32[]{:S(2)}) async-start(), calls=%async_computation.36 | async-start | bytes 655360 | tf_op jit(solution)/shard_map/reduce_scatter | solution.py:195
  134.3 114.2 %reduce-scatter.42.cloned.1.call-start = ((), (), s32[]{:S(2)}) async-start(), calls=%async_computation.34 | async-start | bytes 655360 | tf_op jit(solution)/shard_map/reduce_scatter | solution.py:195
  194.9 2.6 collective-permute-start
  198.7 85.6 %reduce-scatter.44.cloned.1.call-start = ((), (), s32[]{:S(2)}) async-start(), calls=%async_computation.35 | async-start | bytes 655360 | tf_op jit(solution)/shard_map/reduce_scatter | solution.py:195
  266.0 66.5 %reduce-scatter.48.cloned.1.call-start = ((), (), s32[]{:S(2)}) async-start(), calls=%async_computation.37 | async-start | bytes 655360 | tf_op jit(solution)/shard_map/reduce_scatter | solution.py:195
  300.8 2.6 collective-permute-start.1
  304.2 68.3 %reduce-scatter.50.cloned.1.call-start = ((), (), s32[]{:S(2)}) async-start(), calls=%async_computation.38 | async-start | bytes 655360 | tf_op jit(solution)/shard_map/reduce_scatter | solution.py:195
  351.2 73.8 %reduce-scatter.54.cloned.1.call-start = ((), (), s32[]{:S(2)}) async-start(), calls=%async_computation.40 | async-start | bytes 655360 | tf_op jit(solution)/shard_map/reduce_scatter | solution.py:195
  390.8 2.6 collective-permute-start.2
  395.3 69.4 %reduce-scatter.56.cloned.1.call-start = ((), (), s32[]{:S(2)}) async-start(), calls=%async_computation.41 | async-start | bytes 655360 | tf_op jit(solution)/shard_map/reduce_scatter | solution.py:195
  443.4 63.9 %reduce-scatter.58.cloned.1.call-start = ((), (), s32[]{:S(2)}) async-start(), calls=%async_computation.42 | async-start | bytes 655360 | tf_op jit(solution)/shard_map/reduce_scatter | solution.py:203
  486.1 86.0 %reduce-scatter.60.cloned.1.call-start = ((), (), s32[]{:S(2)}) async-start(), calls=%async_computation.43 | async-start | bytes 655360 | tf_op jit(solution)/shard_map/reduce_scatter | solution.py:203
  525.2 23.0 collective-permute-start.3
  550.1 63.6 %reduce-scatter.64.cloned.1.call-start = ((), (), s32[]{:S(2)}) async-start(), calls=%async_computation.45 | async-start | bytes 655360 | tf_op jit(solution)/shard_map/reduce_scatter | solution.py:203
  592.3 85.2 %reduce-scatter.66.cloned.1.call-start = ((), (), s32[]{:S(2)}) async-start(), calls=%async_computation.46 | async-start | bytes 655360 | tf_op jit(solution)/shard_map/reduce_scatter | solution.py:203
  631.6 22.1 collective-permute-start.4
  655.5 64.7 %reduce-scatter.70.cloned.1.call-start = ((), (), s32[]{:S(2)}) async-start(), calls=%async_computation.48 | async-start | bytes 655360 | tf_op jit(solution)/shard_map/reduce_scatter | solution.py:203
  698.9 96.6 %reduce-scatter.100.cloned.1.call-start = ((), (), s32[]{:S(2)}) async-start(), calls=%async_computation.63 | async-start | bytes 557056
  701.8 168.8 %reduce-scatter.102.cloned.1.call-start = ((), (), s32[]{:S(2)}) async-start(), calls=%async_computation.64 | async-start | bytes 557056
  705.0 189.1 %reduce-scatter.72.cloned.1.call-start = ((), (), s32[]{:S(2)}) async-start(), calls=%async_computation.49 | async-start | bytes 655360 | tf_op jit(solution)/shard_map/reduce_scatter | solution.py:203
  736.9 17.4 collective-permute-start.5
  756.2 247.5 %reduce-scatter.104.cloned.1.call-start = ((), (), s32[]{:S(2)}) async-start(), calls=%async_computation.65 | async-start | bytes 557056
  761.3 283.3 %reduce-scatter.94.cloned.1.call-start = ((), (), s32[]{:S(2)}) async-start(), calls=%async_computation.60 | async-start | bytes 557056 | tf_op jit(solution)/shard_map/reduce_scatter | solution.py:183
  767.9 351.4 %reduce-scatter.96.cloned.1.call-start = ((), (), s32[]{:S(2)}) async-start(), calls=%async_computation.61 | async-start | bytes 557056 | tf_op jit(solution)/shard_map/reduce_scatter | solution.py:183
  778.7 415.7 %reduce-scatter.98.cloned.1.call-start = ((), (), s32[]{:S(2)}) async-start(), calls=%async_computation.62 | async-start | bytes 557056 | tf_op jit(solution)/shard_map/reduce_scatter | solution.py:183
  782.8 486.2 %reduce-scatter.88.cloned.1.call-start = ((), (), s32[]{:S(2)}) async-start(), calls=%async_computation.57 | async-start | bytes 278528 | tf_op jit(solution)/shard_map/reduce_scatter | solution.py:180
  801.9 542.1 %reduce-scatter.90.cloned.1.call-start = ((), (), s32[]{:S(2)}) async-start(), calls=%async_computation.58 | async-start | bytes 278528 | tf_op jit(solution)/shard_map/reduce_scatter | solution.py:180
  873.4 545.0 %reduce-scatter.92.cloned.1.call-start = ((), (), s32[]{:S(2)}) async-start(), calls=%async_computation.59 | async-start | bytes 278528 | tf_op jit(solution)/shard_map/reduce_scatter | solution.py:180
  878.1 615.1 %reduce-scatter.82.cloned.1.call-start = ((), (), s32[]{:S(2)}) async-start(), calls=%async_computation.54 | async-start | bytes 139264 | tf_op jit(solution)/shard_map/reduce_scatter | solution.py:177
  949.9 617.6 %reduce-scatter.84.cloned.1.call-start = ((), (), s32[]{:S(2)}) async-start(), calls=%async_computation.55 | async-start | bytes 139264 | tf_op jit(solution)/shard_map/reduce_scatter | solution.py:177
  957.4 684.8 %reduce-scatter.86.cloned.1.call-start = ((), (), s32[]{:S(2)}) async-start(), calls=%async_computation.56 | async-start | bytes 139264 | tf_op jit(solution)/shard_map/reduce_scatter | solution.py:177
  964.7 752.3 %reduce-scatter.80.cloned.1.call-start = ((), (), s32[]{:S(2)}) async-start(), calls=%async_computation.53 | async-start | bytes 417792 | tf_op jit(solution)/shard_map/reduce_scatter | solution.py:174
  976.2 815.9 %reduce-scatter.78.cloned.1.call-start = ((), (), s32[]{:S(2)}) async-start(), calls=%async_computation.52 | async-start | bytes 417792 | tf_op jit(solution)/shard_map/reduce_scatter | solution.py:174
  989.3 877.5 %reduce-scatter.76.cloned.1.call-start = ((), (), s32[]{:S(2)}) async-start(), calls=%async_computation.51 | async-start | bytes 417792 | tf_op jit(solution)/shard_map/reduce_scatter | solution.py:174
  1000.0 890.0 %reduce-scatter.74.cloned.1.call-start = ((), (), s32[]{:S(2)}) async-start(), calls=%async_computation.50 | async-start | bytes 655360 | tf_op jit(solution)/shard_map/reduce_scatter | solution.py:203
  1003.5 416.4 %copy-start.179 = (f32[512]{0:T(512)S(1)}, f32[512]{0:T(512)}, u32[]{:S(2)}) copy-start(f32[512]{0:T(512)} %get-tuple-element.803) | copy-start | bytes 6148
  1003.6 416.4 %copy-start.187 = (f32[512]{0:T(512)S(1)}, f32[512]{0:T(512)}, u32[]{:S(2)}) copy-start(f32[512]{0:T(512)} %get-tuple-element.839) | copy-start | bytes 6148
  1003.6 416.4 %copy-start.178 = (f32[512]{0:T(512)S(1)}, f32[512]{0:T(512)}, u32[]{:S(2)}) copy-start(f32[512]{0:T(512)} %get-tuple-element.778) | copy-start | bytes 6148
  1003.6 416.4 %copy-start.186 = (f32[512]{0:T(512)S(1)}, f32[512]{0:T(512)}, u32[]{:S(2)}) copy-start(f32[512]{0:T(512)} %get-tuple-element.811) | copy-start | bytes 6148
  1003.6 910.1 %reduce-scatter.68.cloned.1.call-start = ((), (), s32[]{:S(2)}) async-start(), calls=%async_computation.47 | async-start | bytes 655360 | tf_op jit(solution)/shard_map/reduce_scatter | solution.py:203
  1195.9 741.9 %copy-start.113 = (f32[1,1,512]{2,0,1:T(1,128)S(1)}, f32[1,1,512]{2,0,1:T(1,128)}, u32[]{:S(2)}) copy-start(f32[1,1,512]{2,0,1:T(1,128)} %copy-done.112) | copy-start | bytes 6148
  1195.9 741.9 %copy-start.154 = (f32[128]{0:T(128)S(1)}, f32[128]{0:T(128)}, u32[]{:S(2)}) copy-start(f32[128]{0:T(128)} %copy-done.153) | copy-start | bytes 1540
  1195.9 741.9 %copy-start.156 = (f32[128]{0:T(128)S(1)}, f32[128]{0:T(128)}, u32[]{:S(2)}) copy-start(f32[128]{0:T(128)} %copy-done.155) | copy-start | bytes 1540
  1195.9 741.8 %copy-start.202 = (f32[128]{0:T(128)S(1)}, f32[128]{0:T(128)}, u32[]{:S(2)}) copy-start(f32[128]{0:T(128)} %copy-done.201) | copy-start | bytes 1540
  1196.0 741.8 %copy-start.221 = (f32[128]{0:T(128)S(1)}, f32[128]{0:T(128)}, u32[]{:S(2)}) copy-start(f32[128]{0:T(128)} %copy-done.220) | copy-start | bytes 1540
  1196.0 741.8 %copy-start.223 = (f32[128]{0:T(128)S(1)}, f32[128]{0:T(128)}, u32[]{:S(2)}) copy-start(f32[128]{0:T(128)} %copy-done.222) | copy-start | bytes 1540
  1196.0 741.8 %copy-start.234 = (f32[128]{0:T(128)S(1)}, f32[128]{0:T(128)}, u32[]{:S(2)}) copy-start(f32[128]{0:T(128)} %copy-done.233) | copy-start | bytes 1540
  1197.2 742.2 %copy-start.196 = (f32[512]{0:T(512)S(1)}, f32[512]{0:T(512)}, u32[]{:S(2)}) copy-start(f32[512]{0:T(512)} %multiply_add_fusion.7) | copy-start | bytes 6148
  1197.2 742.3 %copy-start.198 = (f32[512]{0:T(512)S(1)}, f32[512]{0:T(512)}, u32[]{:S(2)}) copy-start(f32[512]{0:T(512)} %broadcast_multiply_fusion.8) | copy-start | bytes 6148
  1197.2 742.3 %copy-start.200 = (f32[512]{0:T(512)S(1)}, f32[512]{0:T(512)}, u32[]{:S(2)}) copy-start(f32[512]{0:T(512)} %broadcast_multiply_fusion.4) | copy-start | bytes 6148
  1197.2 742.3 %copy-start.197 = (f32[512]{0:T(512)S(1)}, f32[512]{0:T(512)}, u32[]{:S(2)}) copy-start(f32[512]{0:T(512)} %broadcast_multiply_fusion.10) | copy-start | bytes 6148
  1197.3 742.3 %copy-start.199 = (f32[512]{0:T(512)S(1)}, f32[512]{0:T(512)}, u32[]{:S(2)}) copy-start(f32[512]{0:T(512)} %broadcast_multiply_fusion.6) | copy-start | bytes 6148
  1197.3 742.4 %copy-start.243 = (f32[2]{0:T(128)S(1)}, f32[2]{0:T(128)}, u32[]{:S(2)}) copy-start(f32[2]{0:T(128)} %fusion.460) | copy-start | bytes 28
  1197.3 740.5 %reduce-scatter.62.cloned.1.call-start = ((), (), s32[]{:S(2)}) async-start(), calls=%async_computation.44 | async-start | bytes 655360 | tf_op jit(solution)/shard_map/reduce_scatter | solution.py:203
  1419.2 870.2 %copy-start.21 = (f32[128,512]{1,0:T(8,128)S(1)}, f32[128,512]{1,0:T(8,128)}, u32[]{:S(2)}) copy-start(f32[128,512]{1,0:T(8,128)} %get-tuple-element.886) | copy-start | bytes 786436
  1419.2 870.2 %copy-start.63 = (f32[128,512]{1,0:T(8,128)S(1)}, f32[128,512]{1,0:T(8,128)}, u32[]{:S(2)}) copy-start(f32[128,512]{1,0:T(8,128)} %get-tuple-element.876) | copy-start | bytes 786436
  1419.2 870.2 %copy-start.117 = (f32[1,512]{1,0:T(1,128)S(1)}, f32[1,512]{1,0:T(1,128)}, u32[]{:S(2)}) copy-start(f32[1,512]{1,0:T(1,128)} %param.52) | copy-start | bytes 6148
  1419.2 870.2 %copy-start.249 = (f32[128]{0:T(128)S(1)}, f32[128]{0:T(128)}, u32[]{:S(2)}) copy-start(f32[128]{0:T(128)} %broadcast_subtract_fusion.1) | copy-start | bytes 1540
  1421.2 869.5 %copy-start.20 = (f32[128,512]{1,0:T(8,128)S(1)}, f32[128,512]{1,0:T(8,128)}, u32[]{:S(2)}) copy-start(f32[128,512]{1,0:T(8,128)} %get-tuple-element.882) | copy-start | bytes 786436
  1421.2 869.5 %copy-start.48 = (f32[128,512]{1,0:T(8,128)S(1)}, f32[128,512]{1,0:T(8,128)}, u32[]{:S(2)}) copy-start(f32[128,512]{1,0:T(8,128)} %get-tuple-element.872) | copy-start | bytes 786436
  1421.2 869.5 %copy-start.217 = (f32[128]{0:T(128)S(1)}, f32[128]{0:T(128)}, u32[]{:S(2)}) copy-start(f32[128]{0:T(128)} %copy-done.216) | copy-start | bytes 1540
  1421.2 869.5 %copy-start.248 = (f32[128]{0:T(128)S(1)}, f32[128]{0:T(128)}, u32[]{:S(2)}) copy-start(f32[128]{0:T(128)} %broadcast_subtract_fusion) | copy-start | bytes 1540
  (215 other events, 8615.2 us)
Sparse Core Ops, SparseCore 0:
  79.8 19.2 reduce-scatter.51
  131.2 21.0 reduce-scatter.39
  155.3 21.1 reduce-scatter.45
  198.8 26.4 reduce-scatter.41
  266.1 18.1 reduce-scatter.43
  304.4 28.0 reduce-scatter.47
  351.4 21.1 reduce-scatter.49
  395.4 29.6 reduce-scatter.53
  443.5 21.0 reduce-scatter.55
  486.2 21.1 reduce-scatter.57
  550.2 21.8 reduce-scatter.59
  592.5 21.1 reduce-scatter.63
  655.7 21.8 reduce-scatter.65
  699.1 21.1 reduce-scatter.69
  723.3 72.2 reduce-scatter.99
  798.9 71.6 reduce-scatter.101
  873.4 20.6 reduce-scatter.71
  897.1 72.2 reduce-scatter.103
  972.9 71.6 reduce-scatter.93
  1047.6 71.6 reduce-scatter.95
  1122.8 71.6 reduce-scatter.97
  1197.6 71.4 reduce-scatter.87
  1272.5 71.4 reduce-scatter.89
  1347.0 71.3 reduce-scatter.91
  1421.9 71.2 reduce-scatter.81
  1496.3 71.2 reduce-scatter.83
  1570.9 71.2 reduce-scatter.85
  1645.4 71.5 reduce-scatter.79
  1720.5 71.5 reduce-scatter.77
  1795.2 71.5 reduce-scatter.75
  1869.3 20.6 reduce-scatter.73
  1892.5 21.1 reduce-scatter.67
  1916.6 21.1 reduce-scatter.61
where the time goes:
time: 2310 us; the launch traced here: 2300 us
  waiting for transfers between devices  1330 us (58%)
  blocking collectives  702 us (30%)
  matrix products  102 us (4%)
  other arithmetic  78.6 us (3%)
  local copies, waits for them, and re-layouts  48.5 us (2%)
    psum x1, blocking collectives, on_device(): lax.psum((small_sum[0], small_sum[1], small_sum[2], small_sum[3], small_s...  347 us
    reduce_scatter x3, waiting for transfers between devices, spread(): lax.psum_scatter(g_in.astype(jnp.bfloat16), 'dp', scatter_dimension=0, ti...  223 us
    reduce_scatter x3, waiting for transfers between devices, spread(): lax.psum_scatter(g_out.astype(jnp.bfloat16), 'dp', scatter_dimension=1, t...  221 us
    reduce_scatter x3, waiting for transfers between devices, spread(): lax.psum_scatter(g_cross.astype(jnp.bfloat16), 'dp', scatter_dimension=0,...  221 us
    reduce_scatter x3, waiting for transfers between devices, spread(): lax.psum_scatter(g_up.astype(jnp.bfloat16), 'dp', scatter_dimension=0, ti...  189 us
    reduce_scatter x9, waiting for transfers between devices, sums_back(): lax.psum_scatter(value.astype(jnp.bfloat16), 'mp', scatter_dimension=0, t...  187 us
    reduce_scatter x9, waiting for transfers between devices, sums_in(): lax.psum_scatter(value.astype(jnp.bfloat16), 'mp', scatter_dimension=0, t...  153 us
    all_gather x9, blocking collectives, rows_in(): return lax.all_gather(value, 'mp', axis=0, tiled=True)  117 us
  transfers between devices with their start and end apart: 39, of which 36 were waited for; matrix products, arithmetic and copies ran while one was open for 6% of the time, Pallas kernels for 0%

commit v1 on v0

v1 whole, which is shorter than its diff:
```python
import jax
import jax.numpy as jnp
from jax import lax
from jax.experimental import pallas as pl
from jax.experimental.pallas import tpu as pltpu
from jax.sharding import PartitionSpec as P

MESH = pl.DeviceIdType.MESH
BF = jnp.bfloat16
F32 = jnp.float32
EPS = 1e-06
T = 512
SCALE = 0.125
WIDTHS = (512, 1024, 512)

GAIN, SHIFT, UPB, DOWNB, HALTW, SCAL = 0, 3, 6, 10, 11, 12
SMALL = 16

SCRATCH = dict(
    PSB=((32, 512), BF),
    PFB=((32, 1024), BF),
    PCB=((32, 256), BF),
    PK=((SMALL, T), F32),
    HB=((2, 16, 128), BF),
    HL=((4, 16, 128), BF),
    RN=((T, 128), F32),
    IN=((T, T), BF),
    COT=((T, T), BF),
    PSIB=((SMALL, T), F32),
    PV=((SMALL, T), F32),
    W0=((2, 4, 4, 32, 512), BF),
    W1=((2, 4, 4, 32, 1024), BF),
    W2=((2, 4, 4, 32, 512), BF),
    U=((3, T, T), F32),
    F=((3, T, 128), F32),
    N=((3, T, T), BF),
    NT=((3, T, T), BF),
    QKV=((2, T, 384), BF),
    KT=((2, 128, T), BF),
    VT=((2, 128, T), BF),
    HD=((2, T, 128), BF),
    PA=((2, 2, T, T), BF),
    CQ=((2, T, 128), BF),
    CKV=((2, T, 256), BF),
    CKT=((2, 128, T), BF),
    CVT=((2, 128, T), BF),
    HX=((2, T, 128), BF),
    PX=((2, 2, T, T), BF),
    AS=((T, T), F32),
    DIF=((T, T), F32),
    GP=((2, T, T), F32),
    ACT=((2, T, T), BF),
    PB=((2, T, T), BF),
    DA=((T, T), F32),
    DX=((T, T), F32),
    FF=((T, T), BF),
    FB=((T, T), BF),
    LT=((T, T), BF),
    XS=((3, T, T), BF),
    XR=((3, T, T), BF),
    BS=((T, T), F32),
    BX=((T, T), F32),
    MEM=((T, T), BF),
    MT=((T, T), BF),
    DM=((T, T), BF),
    DS=((T, T), BF),
    DSR=((T, T), BF),
    DSO=((T, T), BF),
    DQ=((2, T, 384), BF),
    DH=((2, T, 128), BF),
    DSB=((2, T, T), BF),
    PR=((T, 128), F32),
    OB=((T, T), BF),
    DXB=((T, T), BF),
    G0=((2, 4, 4, 32, 512), BF),
    G1=((2, 4, 4, 32, 1024), BF),
    G2=((2, 4, 4, 32, 512), BF),
    LA0=((2, 3, 4, 32, 512), BF),
    LA1=((2, 3, 4, 32, 1024), BF),
    LA2=((2, 3, 4, 32, 512), BF),
    SA0=((2, 4, 32, 512), BF),
    SA1=((2, 4, 32, 1024), BF),
    SA2=((2, 4, 32, 512), BF),
    LB0=((2, 3, 32, 512), BF),
    LB1=((2, 3, 32, 1024), BF),
    LB2=((2, 3, 32, 512), BF),
    SB0=((2, 32, 512), BF),
    SB1=((2, 32, 1024), BF),
    SB2=((2, 32, 512), BF),
    SM=((SMALL, T), F32),
    LM1=((3, SMALL, T), F32),
    SM2=((SMALL, T), F32),
    LM2=((3, SMALL, T), F32),
    SM3=((SMALL, T), F32),
)

SEMS = dict(
    pp=(1,),
    g0=(2, 4),
    pf=(2,),
    pc=(2, 2),
    po=(2,),
    rk=(2, 2),
    st=(4,),
    hl=(4,),
    ct=(4,),
    lo=(6,),
    ga=(3, 2, 2, 3),
    ex=(3, 4),
    mem=(4, 2),
    mfw=(4,),
    dmx=(4,),
    dme=(4, 2),
    dmf=(4,),
    rs=(3, 2, 2, 3),
    rc=(3, 2),
    os=(2,),
    od=(2,),
    m1=(3,),
    m2=(3,),
    m3=(4,),
)


def mm(a, b):
    return lax.dot_general(a, b, (((1,), (0,)), ((), ())), preferred_element_type=F32)


def mm_nt(a, b):
    return lax.dot_general(a, b, (((1,), (1,)), ((), ())), preferred_element_type=F32)


def mm_tn(a, b):
    return lax.dot_general(a, b, (((0,), (0,)), ((), ())), preferred_element_type=F32)


def rows_of(i, size):
    return pl.ds(pl.multiple_of(i * size, size), size)


def loop(count, body):
    lax.fori_loop(0, count, lambda i, _: (body(i), 0)[1], 0)


def wide(v):
    return jnp.concatenate([v, v, v, v], axis=1)


def mean(v):
    return jnp.mean(v, axis=-1, keepdims=True)


class Refs:
    pass


def kernel(*refs):
    (states, cot, halts, seg, gain, shift, upb, downb, haltw, haltb, w_in, w_out, w_cross, w_up, w_down,
     o_st, o_dx, o_c0, o_c1, o_c2, o_sm) = refs[:21]
    r = Refs()
    rest = refs[21:]
    for name, ref in zip(SCRATCH, rest):
        setattr(r, name, ref)
    rest = rest[len(SCRATCH):]
    ss, rs = {}, {}
    for k, name in enumerate(SEMS):
        ss[name], rs[name] = rest[2 * k], rest[2 * k + 1]
    W, G = (r.W0, r.W1, r.W2), (r.G0, r.G1, r.G2)
    LA, SA = (r.LA0, r.LA1, r.LA2), (r.SA0, r.SA1, r.SA2)
    LB, SB = (r.LB0, r.LB1, r.LB2), (r.SB0, r.SB1, r.SB2)
    LC = (o_c0, o_c1, o_c2)

    c = lax.axis_index("pipe")
    dp = lax.axis_index("dp")
    x = lax.axis_index("mp")
    y, z = dp // 4, lax.rem(dp, 4)
    dec = jnp.logical_or(x == 1, x == 2)
    enc = jnp.logical_not(dec)
    role = jnp.where(dec, 1, 0)
    m = x // 2
    sib = 1 - c
    pair = x + 1 - 2 * lax.rem(x, 2)
    zs = [lax.rem(z + d, 4) for d in range(4)]
    zb = [lax.rem(z + 4 - d, 4) for d in range(4)]
    ys = [lax.rem(y + d, 4) for d in range(4)]
    yb = [lax.rem(y + 4 - d, 4) for d in range(4)]

    def dev(core=c, yy=y, zz=z, xx=x):
        return (core, yy * 4 + zz, xx)

    def rdma(src, dst, ssem, rsem, to):
        return pltpu.make_async_remote_copy(
            src_ref=src, dst_ref=dst, send_sem=ssem, recv_sem=rsem, device_id=to, device_id_type=MESH
        )

    ends = []

    def put(what, when=None):
        rdma(*what()).start()

        def end():
            if when is None:
                rdma(*what()).wait_send()
            else:
                @pl.when(when)
                def _():
                    rdma(*what()).wait_send()

        ends.append(end)

    def put_or_keep(what, when=None):
        def away():
            core, xx = what()[4:]
            return jnp.logical_not(jnp.logical_and(core == c, xx == x))

        @pl.when(jnp.logical_not(away()))
        def _():
            src, dst, _, rsem, _, _ = what()
            pltpu.make_async_copy(src, dst, rsem).start()

        def remote():
            src, dst, ssem, rsem, core, xx = what()
            return rdma(src, dst, ssem, rsem, dev(core, xx=xx))

        @pl.when(away())
        def _():
            remote().start()

        def end():
            out = away()
            if when is not None:
                out = jnp.logical_and(out, when)

            @pl.when(out)
            def _():
                remote().wait_send()

        ends.append(end)

    def got(dst, rsem):
        pltpu.make_async_copy(dst, dst, rsem).wait()

    barrier = pltpu.get_barrier_semaphore()
    partners = [dev(zz=zs[d]) for d in (1, 2, 3)] + [dev(yy=ys[d]) for d in (1, 2, 3)]
    partners += [dev(core=sib, xx=lax.rem(x + d, 4)) for d in range(4)]
    partners += [dev(xx=lax.rem(x + d, 4)) for d in (1, 2, 3)]
    jj_me = lax.rem(x, 2)
    to_y = [jnp.where(jj_me == 0, y, ys[d]) for d in range(4)]
    to_z = [jnp.where(jj_me == 0, zs[d], z) for d in range(4)]
    for d in (1, 2, 3):
        partners.append(dev(core=role, zz=zb[d], xx=2 * c))
        partners.append(dev(core=role, yy=yb[d], xx=2 * c + 1))
    for to in partners:
        pl.semaphore_signal(barrier, inc=1, device_id=to, device_id_type=MESH)

    staged = [
        (w_in.at[0], r.PSB.at[:, pl.ds(0, 128)]), (w_in.at[1], r.PSB.at[:, pl.ds(128, 128)]),
        (w_in.at[2], r.PSB.at[:, pl.ds(256, 128)]), (w_out, r.PSB.at[:, pl.ds(384, 128)]),
        (w_up, r.PFB.at[:, pl.ds(0, 512)]), (w_down, r.PFB.at[:, pl.ds(512, 512)])]
    staged = [pltpu.make_async_copy(a, b, rs["lo"].at[k]) for k, (a, b) in enumerate(staged)]
    for copy in staged:
        copy.start()
    r.PK[GAIN:GAIN + 3] = gain[:, 0, :]
    r.PK[SHIFT:SHIFT + 3] = shift[:, 0, :]
    r.PK[UPB:UPB + 4] = upb[:, 0, :]
    r.PK[DOWNB:DOWNB + 1] = downb[...]
    r.PK[HALTW:HALTW + 1] = haltw[...]
    r.PK[SCAL:SCAL + 1] = jnp.broadcast_to(haltb[...], (1, T))
    r.PK[SCAL + 1:SMALL] = jnp.zeros((SMALL - SCAL - 1, T), F32)
    for k in (0, 1):
        r.HB[k] = jnp.broadcast_to(halts[k:k + 1].astype(F32), (16, 128)).astype(BF)
    crossed = w_cross[...].astype(F32)
    for k in (0, 1):
        r.PCB[:, 128 * k:128 * k + 128] = crossed[:, k, :].astype(BF)
    for copy in staged:
        copy.wait()
    pl.semaphore_wait(barrier, len(partners))

    homes = (c, 3 - c)

    def gather_first(g):
        for d in (1, 2, 3):
            put(lambda d=d: (W[g].at[0, y, z], W[g].at[0, y, z], ss["ga"].at[g, 0, 0, d - 1], rs["ga"].at[g, 0, 0, d - 1], dev(zz=zs[d])), dec if g == 2 else None)
            put(lambda d=d: (W[g].at[1, y, z], W[g].at[1, y, z], ss["ga"].at[g, 0, 1, d - 1], rs["ga"].at[g, 0, 1, d - 1], dev(yy=ys[d])), dec if g == 2 else None)

    def gather_second(g):
        for d in range(4):
            if g == 0:
                got(W[g].at[0, y, zb[d]], rs["g0"].at[0, d])
                got(W[g].at[1, yb[d], z], rs["g0"].at[1, d])
            elif d > 0:
                got(W[g].at[0, y, zb[d]], rs["ga"].at[g, 0, 0, d - 1])
                got(W[g].at[1, yb[d], z], rs["ga"].at[g, 0, 1, d - 1])
        for d in (1, 2, 3):
            put(lambda d=d: (W[g].at[0, y], W[g].at[0, y], ss["ga"].at[g, 1, 0, d - 1], rs["ga"].at[g, 1, 0, d - 1], dev(yy=ys[d])), dec if g == 2 else None)
            put(lambda d=d: (W[g].at[1, :, z], W[g].at[1, :, z], ss["ga"].at[g, 1, 1, d - 1], rs["ga"].at[g, 1, 1, d - 1], dev(zz=zs[d])), dec if g == 2 else None)

    def gather_done(g):
        for d in (1, 2, 3):
            got(W[g].at[0, yb[d]], rs["ga"].at[g, 1, 0, d - 1])
            got(W[g].at[1, :, zb[d]], rs["ga"].at[g, 1, 1, d - 1])

    def reduce_first(g, jj, when=None):
        for d in (1, 2, 3):
            def what(d=d):
                src, to = (G[g].at[0, ys[d]], dev(yy=ys[d])) if jj == 0 else (G[g].at[1, :, zs[d]], dev(zz=zs[d]))
                return src, LA[g].at[jj, d - 1], ss["rs"].at[g, 0, jj, d - 1], rs["rs"].at[g, 0, jj, d - 1], to

            put(what, when)

    def reduce_second(g):
        for jj in (0, 1):
            for d in (1, 2, 3):
                got(LA[g].at[jj, d - 1], rs["rs"].at[g, 0, jj, d - 1])

            def add(k):
                own = G[g][0, y, k] if jj == 0 else G[g][1, k, z]
                total = own.astype(F32)
                for d in range(3):
                    total = total + LA[g][jj, d, k].astype(F32)
                SA[g][jj, k] = total.astype(BF)

            loop(4, add)
            for d in (1, 2, 3):
                def what(d=d, jj=jj):
                    src, to = (SA[g].at[0, zs[d]], dev(zz=zs[d])) if jj == 0 else (SA[g].at[1, ys[d]], dev(yy=ys[d]))
                    return src, LB[g].at[jj, d - 1], ss["rs"].at[g, 1, jj, d - 1], rs["rs"].at[g, 1, jj, d - 1], to

                put(what, dec if g == 2 else None)

    def reduce_third(g):
        for jj in (0, 1):
            for d in (1, 2, 3):
                got(LB[g].at[jj, d - 1], rs["rs"].at[g, 1, jj, d - 1])
            total = (SA[g][0, z] if jj == 0 else SA[g][1, y]).astype(F32)
            for d in range(3):
                total = total + LB[g][jj, d].astype(F32)
            SB[g][jj] = total.astype(BF)
            if g == 2:
                for k in (0, 1):
                    put_or_keep(lambda jj=jj, k=k: (
                        SB[g].at[jj, :, pl.ds(256 * k, 256)], LC[g].at[m], ss["rk"].at[k, jj], rs["rc"].at[g, m],
                        k, 2 * c + jj), dec)
            else:
                put_or_keep(lambda jj=jj: (
                    SB[g].at[jj], LC[g].at[m], ss["rc"].at[g, jj], rs["rc"].at[g, m], role, 2 * c + jj))

    def half_rows(i, core):
        return pl.ds(pl.multiple_of(128 * i + 64 * core, 64), 64)

    def memory_copy(i):
        part = half_rows(i, c)
        return rdma(r.N.at[1, part], r.MEM.at[part], ss["mem"].at[i, 0], rs["mem"].at[i, c], dev(xx=pair))

    def memory_forward(i):
        part = half_rows(i, c)
        return rdma(r.MEM.at[part], r.MEM.at[part], ss["mfw"].at[i], rs["mem"].at[i, c], dev(core=sib))

    def memory_grad_swap(i):
        part = half_rows(i, sib)
        return rdma(r.DS.at[part], r.DSR.at[part], ss["dmx"].at[i], rs["dmx"].at[i], dev(core=sib))

    def memory_grad_copy(i):
        part = half_rows(i, c)
        return rdma(r.DSO.at[part], r.DM.at[part], ss["dme"].at[i, 0], rs["dme"].at[i, c], dev(xx=pair))

    def memory_grad_forward(i):
        part = half_rows(i, c)
        return rdma(r.DM.at[part], r.DM.at[part], ss["dmf"].at[i], rs["dme"].at[i, c], dev(core=sib))

    def exchange_copy(k, i):
        part = rows_of(i, 128)
        return rdma(r.XS.at[k, part], r.XR.at[k, part], ss["ex"].at[k, i], rs["ex"].at[k, i], dev(core=sib))

    for d in range(4):
        for k in (0, 1):
            if d == 0:
                put_or_keep(lambda k=k: (
                    r.PSB, r.W0.at[jj_me, y, z], ss["g0"].at[k, 0], rs["g0"].at[jj_me, 0], x // 2, homes[k]))
            else:
                put(lambda k=k, d=d: (
                    r.PSB, r.W0.at[jj_me, y, z], ss["g0"].at[k, d], rs["g0"].at[jj_me, d],
                    dev(core=x // 2, yy=to_y[d], zz=to_z[d], xx=homes[k])))
    for k in (0, 1):
        put_or_keep(lambda k=k: (
            r.PFB, r.W1.at[jj_me, y, z], ss["pf"].at[k], rs["pf"].at[jj_me], x // 2, homes[k]))
    put(lambda: (r.PK, r.PSIB, ss["pp"].at[0], rs["pp"].at[0], dev(core=sib)))
    r.SM[...] = jnp.zeros((SMALL, T), F32)
    for jj in (0, 1):
        got(r.W1.at[jj, y, z], rs["pf"].at[jj])
    gather_first(1)
    for k in (0, 1):
        for core in (0, 1):
            put_or_keep(lambda k=k, core=core: (
                states.at[k], r.IN.at[rows_of(x, 128)], ss["st"].at[2 * k + core], rs["st"].at[x], core, homes[k]))
            put_or_keep(lambda k=k, core=core: (
                r.HB.at[k], r.HL.at[x], ss["hl"].at[2 * k + core], rs["hl"].at[x], core, homes[k]))
    gather_second(0)
    for k in (0, 1):
        put_or_keep(lambda k=k: (
            r.PCB, r.W2.at[jj_me, y, z, :, pl.ds(pl.multiple_of(256 * c, 256), 256)], ss["po"].at[k],
            rs["pc"].at[jj_me, c], x // 2, k + 1))
    gather_second(1)
    for k in (0, 1):
        for core in (0, 1):
            put_or_keep(lambda k=k, core=core: (
                cot.at[k], r.COT.at[rows_of(x, 128)], ss["ct"].at[2 * k + core], rs["ct"].at[x], core, homes[k]))
    got(r.PSIB, rs["pp"].at[0])
    r.PV[...] = jnp.where(c == role, r.PK[...], r.PSIB[...])
    for q in range(4):
        got(r.IN.at[pl.ds(128 * q, 128)], rs["st"].at[q])
        got(r.HL.at[q], rs["hl"].at[q])

    def param(row):
        return r.PV[pl.ds(row, 1), :]

    def ln_to(li, part, size, v):
        center = v - mean(v)
        factor = lax.rsqrt(mean(center * center) + EPS)
        unit = center * factor
        normed = unit * param(GAIN + li) + param(SHIFT + li)
        r.U[li, part] = unit
        r.F[li, part] = jnp.broadcast_to(factor, (size, 128))
        r.N[li, part] = normed.astype(BF)

    def count(row, v):
        r.SM[pl.ds(row, 1), :] += jnp.sum(v, axis=0, keepdims=True)

    def ln_back(li, part, n):
        unit, factor = r.U[li, part], wide(r.F[li, part])
        scaled = n * param(GAIN + li)
        count(GAIN + li, n * unit)
        count(SHIFT + li, n)
        return factor * (scaled - mean(scaled) - unit * mean(scaled * unit))

    def weight(g, jj, lo, hi):
        return W[g][jj, :, :, :, lo:hi].reshape(T, hi - lo)

    def both(g, lo, hi):
        return jnp.concatenate([weight(g, 0, lo, hi), weight(g, 1, lo, hi)], axis=1)

    def send_part(k, i, size, value):
        r.XS[k, rows_of(i, size)] = value.astype(BF)
        for h in range(size // 128):
            exchange_copy(k, i * (size // 128) + h).start()

    def received(k, part):
        return r.XS[k, part].astype(F32) + r.XR[k, part].astype(F32)

    def after_exchange(k, i, body):
        def one(h):
            exchange_copy(k, 2 * i + h).wait()
            body(rows_of(2 * i + h, 128))

        loop(2, one)

    low_lane = lax.broadcasted_iota(jnp.int32, (1, 128), 1) < 64

    def head_part(v, hh):
        return jnp.where(low_lane if hh == 0 else jnp.logical_not(low_lane), v, jnp.zeros_like(v))

    def attend(q_of, kv, k_at, vt, bias, probs, heads):
        for jj in (0, 1):
            q, keys = q_of(jj), kv[jj, :, k_at:k_at + 128]
            outs = []
            for hh in (0, 1):
                s = mm_nt(keys, head_part(q, hh)) + bias[...]
                e = jnp.exp(s - jnp.max(s, axis=0, keepdims=True))
                w = (e * (1.0 / jnp.sum(e, axis=0, keepdims=True))).astype(BF)
                probs[jj, hh] = w
                outs.append(mm(vt[jj, 64 * hh:64 * hh + 64, :], w))
            heads[jj] = jnp.concatenate(outs, axis=0).T.astype(BF)

    def attend_back(q_of, kv, v_at, kt, probs, dq_at, dk_at, dv_at):
        for jj in (0, 1):
            q, o, values = q_of(jj), r.DH[jj], kv[jj, :, v_at:v_at + 128]
            for hh in (0, 1):
                w = probs[jj, hh].astype(F32)
                wd = w * mm_nt(values, head_part(o, hh))
                delta = jnp.sum(wd, axis=0, keepdims=True)
                r.DSB[hh] = (wd - w * delta).astype(BF)
            dks = [mm(r.DSB[hh], q) for hh in (0, 1)]
            dvs = [mm(probs[jj, hh], o) for hh in (0, 1)]
            dqs = [mm(kt[jj, 64 * hh:64 * hh + 64, :], r.DSB[hh]) for hh in (0, 1)]
            r.DQ[jj, :, dk_at:dk_at + 128] = jnp.where(low_lane, dks[0], dks[1]).astype(BF)
            r.DQ[jj, :, dv_at:dv_at + 128] = jnp.where(low_lane, dvs[0], dvs[1]).astype(BF)
            r.DQ[jj, :, dq_at:dq_at + 128] = (jnp.concatenate(dqs, axis=0).T * SCALE).astype(BF)

    def flip(target, source):
        def one(i):
            part = rows_of(i, 128)
            target[part, :] = source[:, part].T

        loop(4, one)

    def outer(g, jj, lo, hi, left_t, right):
        def one(h):
            total = mm(left_t[rows_of(h, 256), :], right())
            G[g][jj, pl.ds(2 * h, 2), :, :, lo:hi] = total.astype(BF).reshape(2, 4, 32, hi - lo)

        loop(2, one)

    def first(i):
        part = rows_of(i, 128)
        v = r.IN[part].astype(F32)
        ln_to(0, part, 128, v)
        logit = jnp.sum(v * param(HALTW), axis=-1, keepdims=True) + param(SCAL)[:, 0:1]
        r.PR[part] = jnp.broadcast_to(jax.nn.sigmoid(logit), (128, 128))
        r.RN[part] = mm_tn(r.HL[i], jnp.full((16, 128), 1.0 / 16.0, BF))

    loop(4, first)

    docs = lax.broadcasted_iota(jnp.int32, (16, T), 0)
    seg_src, seg_tgt = seg[0, pl.ds(m, 1), :], seg[1, pl.ds(m, 1), :]
    own_src = jnp.where(docs == seg_src, 1.0, 0.0).astype(BF)
    own_tgt = jnp.where(docs == seg_tgt, 1.0, 0.0).astype(BF)
    own_self = jnp.where(enc, own_src, own_tgt)
    k_at = lax.broadcasted_iota(jnp.int32, (T, T), 1)
    q_at = lax.broadcasted_iota(jnp.int32, (T, T), 0)
    reach = jnp.where(enc, T, 0)
    same = jnp.logical_and(mm_tn(own_self, own_self) > 0.5, q_at <= k_at + reach)
    r.BS[...] = jnp.where(same, 0.0, -1e30)

    @pl.when(dec)
    def _():
        r.BX[...] = jnp.where(mm_tn(own_src, own_tgt) > 0.5, 0.0, -1e30)

    @pl.when(dec)
    def _():
        for jj in (0, 1):
            for k in (0, 1):
                got(r.W2.at[jj, y, z, :, pl.ds(256 * k, 256)], rs["pc"].at[jj, k])
        gather_first(2)

    gather_done(0)

    for jj in (0, 1):
        def project(i):
            part = rows_of(i, 256)
            three = mm(r.N[0, part], weight(0, jj, 0, 384))
            r.QKV[jj, part, 0:128] = (three[:, 0:128] * SCALE).astype(BF)
            r.QKV[jj, part, 128:384] = three[:, 128:384].astype(BF)
            r.KT[jj, :, part] = three[:, 128:256].T.astype(BF)
            r.VT[jj, :, part] = three[:, 256:384].T.astype(BF)

        loop(2, project)

    attend(lambda jj: r.QKV[jj, :, 0:128], r.QKV, 128, r.VT, r.BS, r.PA, r.HD)

    @pl.when(dec)
    def _():
        gather_second(2)

    def self_out(i):
        part = rows_of(i, 256)
        heads = jnp.concatenate([r.HD[0, part], r.HD[1, part]], axis=1)
        send_part(0, i, 256, mm_nt(heads, both(0, 384, 512)))

    loop(2, self_out)
    second = jnp.where(enc, 2, 1)

    def self_after(part):
        v = r.IN[part].astype(F32) + received(0, part)
        r.AS[part] = v
        ln_to(second, part, 128, v)

    @pl.when(dec)
    def _():
        gather_done(2)
        loop(2, lambda i: after_exchange(0, i, self_after))
        for jj in (0, 1):
            def ask(i):
                part = rows_of(i, 256)
                r.CQ[jj, part] = (mm(r.N[1, part], weight(2, jj, 256, 384)) * SCALE).astype(BF)

            loop(2, ask)
        flip(r.NT.at[0], r.N.at[0])

        def memory_in(i):
            @pl.when(i < 4)
            def _():
                got(r.MEM.at[half_rows(i, c)], rs["mem"].at[i, c])
                memory_forward(i).start()

            @pl.when(i > 0)
            def _():
                j = i - 1
                got(r.MEM.at[half_rows(j, sib)], rs["mem"].at[j, sib])
                part = rows_of(j, 128)
                for jj in (0, 1):
                    pairs = mm(r.MEM[part], weight(2, jj, 0, 256))
                    r.CKV[jj, part] = pairs.astype(BF)
                    r.CKT[jj, :, part] = pairs[:, 0:128].T.astype(BF)
                    r.CVT[jj, :, part] = pairs[:, 128:256].T.astype(BF)

        loop(5, memory_in)
        attend(lambda jj: r.CQ[jj], r.CKV, 0, r.CVT, r.BX, r.PX, r.HX)

        def cross_out(i):
            part = rows_of(i, 256)
            heads = jnp.concatenate([r.HX[0, part], r.HX[1, part]], axis=1)
            send_part(2, i, 256, mm_nt(heads, both(2, 384, 512)))

        loop(2, cross_out)

    gather_done(1)

    def cross_after(part):
        v = r.AS[part] + received(2, part)
        r.AS[part] = v
        ln_to(2, part, 128, v)

    def ffn(i):
        pl.when(enc)(lambda: after_exchange(0, i, self_after))
        pl.when(dec)(lambda: after_exchange(2, i, cross_after))
        part = rows_of(i, 256)
        total = None
        for jj in (0, 1):
            bias = r.PV[pl.ds(UPB + 2 * c + jj, 1), :]
            u = mm(r.N[2, part], weight(1, jj, 0, 512)) + bias
            sq = u * u
            t = jnp.tanh(0.7978845608028654 * (u + 0.044715 * sq * u))
            r.GP[jj, part] = 0.5 * (1.0 + t) + 0.5 * u * (1.0 - t * t) * (
                0.7978845608028654 * (1.0 + 3 * 0.044715 * sq))
            act = (0.5 * u * (1.0 + t)).astype(BF)
            r.ACT[jj, part] = act
            term = mm_nt(act, weight(1, jj, 512, 1024))
            total = term if total is None else total + term
        send_part(1, i, 256, total)

    loop(2, ffn)

    def running(part):
        mask = r.RN[part]
        return mask, mask * r.PR[part]

    def ffn_after(part):
        v = r.IN[part].astype(F32)
        diff = r.AS[part] + received(1, part) + param(DOWNB) - v
        r.DIF[part] = diff
        mask, run = running(part)
        lane = lax.broadcasted_iota(jnp.int32, (1, 128), 1)
        tally = jnp.where(lane == 1, run, jnp.where(lane == 2, mask, 0.0))
        r.SM[SCAL:SCAL + 1, 0:128] += jnp.sum(tally, axis=0, keepdims=True)
        return v + wide(run) * diff

    @pl.when(enc)
    def _():
        def memory_out(i):
            exchange_copy(1, i).wait()
            part = rows_of(i, 128)
            ln_to(1, part, 128, ffn_after(part))
            memory_copy(i).start()

        loop(4, memory_out)
        r.OB[...] = r.N[1]

    for q in range(4):
        got(r.COT.at[pl.ds(128 * q, 128)], rs["ct"].at[q])

    def halt_back(part, g):
        v = r.IN[part].astype(F32)
        mask, run = running(part)
        prob = r.PR[part]
        run = wide(run)
        d_aff = g * run
        r.DA[part] = d_aff
        r.FF[part] = d_aff.astype(BF)
        dot = jnp.sum(g * r.DIF[part], axis=-1, keepdims=True)
        zz = mask * dot * prob * (1.0 - prob)
        zw = wide(zz)
        r.DX[part] = g * (1.0 - run) + zw * param(HALTW)
        count(DOWNB, d_aff)
        count(HALTW, zw * v)
        lane = lax.broadcasted_iota(jnp.int32, (1, 128), 1)
        r.SM[SCAL:SCAL + 1, 0:128] += jnp.sum(jnp.where(lane == 0, zz, 0.0), axis=0, keepdims=True)

    def memory_grad_pass(i):
        for h in (0, 1):
            got(r.DM.at[half_rows(2 * i + h, c)], rs["dme"].at[2 * i + h, c])
            memory_grad_forward(2 * i + h).start()

    def memory_grad_in(i):
        def one(h):
            j = 2 * i + h
            got(r.DM.at[half_rows(j, sib)], rs["dme"].at[j, sib])
            part = rows_of(j, 128)
            n = r.COT[part].astype(F32) + r.DM[part].astype(F32)
            halt_back(part, ln_back(1, part, n))

        loop(2, one)
        pl.when(i == 0)(lambda: memory_grad_pass(1))

    def output_in(i):
        def one(h):
            exchange_copy(1, 2 * i + h).wait()
            part = rows_of(2 * i + h, 128)
            r.OB[part] = ffn_after(part).astype(BF)
            halt_back(part, r.COT[part].astype(F32))

        loop(2, one)

    @pl.when(enc)
    def _():
        flip(r.NT.at[2], r.N.at[2])
        flip(r.NT.at[0], r.N.at[0])
        memory_grad_pass(0)

    def ffn_back(i):
        pl.when(enc)(lambda: memory_grad_in(i))
        pl.when(dec)(lambda: output_in(i))
        part = rows_of(i, 256)
        total = None
        for jj in (0, 1):
            dp_ = mm(r.FF[part], weight(1, jj, 512, 1024)) * r.GP[jj, part]
            row = UPB + 2 * c + jj
            r.SM[pl.ds(row, 1), :] += jnp.sum(dp_, axis=0, keepdims=True)
            low = dp_.astype(BF)
            r.PB[jj, part] = low
            term = mm_nt(low, weight(1, jj, 0, 512))
            total = term if total is None else total + term
        send_part(0, i, 256, total)

    loop(2, ffn_back)
    for h in (0, 1):
        quarter = 2 * c + h
        put_or_keep(lambda h=h, quarter=quarter: (
            r.OB.at[rows_of(quarter, 128)], o_st.at[m], ss["os"].at[h], rs["os"].at[m], role, quarter))

    def ffn_weights(when):
        flip(r.LT, r.FF)
        for jj in (0, 1):
            outer(1, jj, 0, 512, r.NT.at[2], lambda: r.PB[jj])
            outer(1, jj, 512, 1024, r.LT, lambda: r.ACT[jj])
            reduce_first(1, jj, when)

    pl.when(enc)(lambda: ffn_weights(enc))

    def ffn_back_after(part):
        d = r.DA[part] + ln_back(2, part, received(0, part))
        r.DA[part] = d
        r.FB[part] = d.astype(BF)

    def heads_back(g, i):
        part = rows_of(i, 256)
        both_heads = mm(r.FB[part], both(g, 384, 512)).astype(BF)
        r.DH[0, part], r.DH[1, part] = both_heads[:, 0:128], both_heads[:, 128:256]

    def after_ffn_back(i):
        after_exchange(0, i, ffn_back_after)
        pl.when(enc)(lambda: heads_back(0, i))
        pl.when(dec)(lambda: heads_back(2, i))

    loop(2, after_ffn_back)

    @pl.when(dec)
    def _():
        attend_back(lambda jj: r.CQ[jj], r.CKV, 128, r.CKT, r.PX, 256, 0, 128)

        def memory_back(i):
            part = rows_of(i, 128)
            pairs = jnp.concatenate([r.DQ[0, part, 0:256], r.DQ[1, part, 0:256]], axis=1)
            r.DS[part] = mm_nt(pairs, both(2, 0, 256)).astype(BF)
            memory_grad_swap(i).start()

        loop(4, memory_back)

        def memory_grad_out(i):
            part = half_rows(i, c)
            got(r.DSR.at[part], rs["dmx"].at[i])
            r.DSO[part] = (r.DS[part].astype(F32) + r.DSR[part].astype(F32)).astype(BF)
            memory_grad_copy(i).start()

        loop(4, memory_grad_out)
        flip(r.NT.at[2], r.N.at[2])
        ffn_weights(dec)

        def query_back(i):
            part = rows_of(i, 256)
            asked = jnp.concatenate([r.DQ[0, part, 256:384], r.DQ[1, part, 256:384]], axis=1)
            send_part(1, i, 256, mm_nt(asked, both(2, 256, 384)))

        loop(2, query_back)
        flip(r.LT, r.FB)
        flip(r.NT.at[1], r.N.at[1])
        flip(r.MT, r.MEM)
        for jj in (0, 1):
            outer(2, jj, 0, 256, r.MT, lambda: r.DQ[jj, :, 0:256])
            outer(2, jj, 256, 384, r.NT.at[1], lambda: r.DQ[jj, :, 256:384])
            outer(2, jj, 384, 512, r.LT, lambda: r.HX[jj])
            reduce_first(2, jj, dec)

        def cross_back_after(part):
            d = r.DA[part] + ln_back(1, part, received(1, part))
            r.DA[part] = d
            r.FB[part] = d.astype(BF)

        def after_query_back(i):
            after_exchange(1, i, cross_back_after)
            heads_back(0, i)

        loop(2, after_query_back)

    flip(r.LT, r.FB)
    for jj in (0, 1):
        outer(0, jj, 384, 512, r.LT, lambda: r.HD[jj])
    attend_back(lambda jj: r.QKV[jj, :, 0:128], r.QKV, 256, r.KT, r.PA, 0, 128, 256)

    for jj in (0, 1):
        outer(0, jj, 0, 384, r.NT.at[0], lambda: r.DQ[jj])
        reduce_first(0, jj)

    def first_back(i):
        part = rows_of(i, 256)
        all_three = jnp.concatenate([r.DQ[0, part], r.DQ[1, part]], axis=1)
        send_part(2, i, 256, mm_nt(all_three, both(0, 0, 384)))

    loop(2, first_back)

    def first_back_after(part):
        d = r.DX[part] + r.DA[part] + ln_back(0, part, received(2, part))
        r.DXB[part] = d.astype(BF)

    loop(2, lambda i: after_exchange(2, i, first_back_after))
    for h in (0, 1):
        quarter = 2 * c + h
        put_or_keep(lambda h=h, quarter=quarter: (r.DXB.at[rows_of(quarter, 128)], o_dx.at[m], ss["od"].at[h], rs["od"].at[m], role, quarter))

    row_id = lax.broadcasted_iota(jnp.int32, (SMALL, T), 0)
    halves = jnp.logical_and(row_id >= UPB, row_id < DOWNB)
    r.SM2[...] = jnp.where(jnp.logical_or(halves, c == 0), r.SM[...], 0.0)
    for d in (1, 2, 3):
        put(lambda d=d: (r.SM2, r.LM1.at[d - 1], ss["m1"].at[d - 1], rs["m1"].at[d - 1], dev(zz=zs[d])))
    reduce_second(1)

    @pl.when(dec)
    def _():
        reduce_second(2)

    for d in range(3):
        got(r.LM1.at[d], rs["m1"].at[d])
    r.SM3[...] = r.SM2[...] + r.LM1[0] + r.LM1[1] + r.LM1[2]
    for d in (1, 2, 3):
        put(lambda d=d: (r.SM3, r.LM2.at[d - 1], ss["m2"].at[d - 1], rs["m2"].at[d - 1], dev(yy=ys[d])))

    reduce_second(0)
    reduce_third(1)

    @pl.when(dec)
    def _():
        reduce_third(2)

    for d in range(3):
        got(r.LM2.at[d], rs["m2"].at[d])
    r.SM[...] = r.SM3[...] + r.LM2[0] + r.LM2[1] + r.LM2[2]
    for k in range(4):
        put_or_keep(lambda k=k: (r.SM, o_sm.at[2 * m + c], ss["m3"].at[k], rs["m3"].at[2 * m + c], role, k))
    reduce_third(0)
    for k in range(4):
        got(o_sm.at[k], rs["m3"].at[k])
    for k in (0, 1):
        got(o_st.at[k], rs["os"].at[k])
        got(o_dx.at[k], rs["od"].at[k])
        for g in range(3):
            got(LC[g].at[k], rs["rc"].at[g, k])

    @pl.when(enc)
    def _():
        for i in range(4):
            memory_copy(i).wait_send()
            memory_grad_forward(i).wait_send()

    @pl.when(dec)
    def _():
        for i in range(4):
            memory_forward(i).wait_send()
            memory_grad_swap(i).wait_send()
            memory_grad_copy(i).wait_send()

    for end in ends:
        end()


def finish(st, dx, c0, c1, c2, small, o_st, o_dx, o_gain, o_shift, o_in, o_out, o_cross, o_up, o_upb, o_down, o_downb,
           o_haltw, o_haltb, o_act):
    o_st[...] = st[...]
    o_dx[...] = dx[...].astype(F32)
    both = c0[0].astype(F32) + c0[1].astype(F32)
    for k in range(3):
        o_in[k] = both[:, 128 * k:128 * k + 128]
    o_out[...] = both[:, 384:512]
    both = c1[0].astype(F32) + c1[1].astype(F32)
    o_up[...], o_down[...] = both[:, 0:512], both[:, 512:1024]
    both = c2[0].astype(F32) + c2[1].astype(F32)
    for k in (0, 1):
        o_cross[:, k, :] = both[:, 128 * k:128 * k + 128]
    total = small[0] + small[1] + small[2] + small[3]
    for k in range(3):
        o_gain[k] = total[GAIN + k:GAIN + k + 1]
        o_shift[k] = total[SHIFT + k:SHIFT + k + 1]
    for k in range(4):
        o_upb[:, 512 * k:512 * k + 512] = total[UPB + k:UPB + k + 1]
    o_downb[...] = total[DOWNB:DOWNB + 1]
    o_haltw[...] = total[HALTW:HALTW + 1]
    o_haltb[...] = total[SCAL:SCAL + 1, 0:1]
    ran, alive = total[SCAL:SCAL + 1, 1:2], total[SCAL:SCAL + 1, 2:3]
    o_act[...] = jnp.concatenate([ran / alive, 1.0 - alive / (32 * T)], axis=1)


def on_device(states, cotangent, halting, segments, norm_gain, norm_bias, attn_in, attn_out, cross, up_weight, up_bias,
              down_weight, down_bias, halt_weight, halt_bias):
    vm, anywhere = pl.BlockSpec(memory_space=pltpu.VMEM), pl.BlockSpec(memory_space=pl.ANY)
    arrived = pl.pallas_call(
        kernel,
        out_shape=[
            jax.ShapeDtypeStruct((2, 128, T), BF),
            jax.ShapeDtypeStruct((2, 128, T), BF),
            jax.ShapeDtypeStruct((2, 32, 512), BF),
            jax.ShapeDtypeStruct((2, 32, 1024), BF),
            jax.ShapeDtypeStruct((2, 32, 256), BF),
            jax.ShapeDtypeStruct((4, SMALL, T), F32),
        ],
        in_specs=[anywhere] * 2 + [vm] * 8 + [anywhere] * 2 + [vm] + [anywhere] * 2,
        out_specs=[anywhere] * 6,
        scratch_shapes=[pltpu.VMEM(*spec) for spec in SCRATCH.values()]
        + [pltpu.SemaphoreType.DMA(shape) for shape in SEMS.values() for _ in (0, 1)],
        compiler_params=pltpu.CompilerParams(
            collective_id=0, has_side_effects=True, vmem_limit_bytes=62 * 2**20),
        name="step",
    )(states[0], cotangent[0], halting[0], segments, jnp.transpose(norm_gain, (1, 0, 2)),
      jnp.transpose(norm_bias, (1, 0, 2)), up_bias.reshape(4, 1, T), down_bias, halt_weight,
      halt_bias.reshape(1, 1), jnp.transpose(attn_in[0], (1, 0, 2)), attn_out[0].T, cross[0], up_weight[0],
      down_weight[0].T)
    st, dx, gain, shift, g_in, g_out, g_cross, g_up, upb, g_down, downb, haltw, haltb, act = pl.pallas_call(
        finish,
        out_shape=[
            jax.ShapeDtypeStruct((2, 128, T), BF),
            jax.ShapeDtypeStruct((2, 128, T), F32),
            jax.ShapeDtypeStruct((3, 1, T), F32),
            jax.ShapeDtypeStruct((3, 1, T), F32),
            jax.ShapeDtypeStruct((3, 32, 128), F32),
            jax.ShapeDtypeStruct((32, 128), F32),
            jax.ShapeDtypeStruct((32, 2, 128), F32),
            jax.ShapeDtypeStruct((32, 512), F32),
            jax.ShapeDtypeStruct((1, 2048), F32),
            jax.ShapeDtypeStruct((32, 512), F32),
            jax.ShapeDtypeStruct((1, T), F32),
            jax.ShapeDtypeStruct((1, T), F32),
            jax.ShapeDtypeStruct((1, 1), F32),
            jax.ShapeDtypeStruct((1, 2), F32),
        ],
        in_specs=[vm] * 6,
        out_specs=[vm] * 14,
        name="finish",
    )(*arrived)
    return (
        st[None], dx[None], jnp.transpose(gain, (1, 0, 2)), jnp.transpose(shift, (1, 0, 2)),
        jnp.transpose(g_in, (1, 0, 2))[None], g_out.T[None], g_cross[None], g_up[None], upb, g_down.T[None], downb,
        haltw, haltb.reshape(1), act,
    )


def solution(mesh):
    split = (
        P("pipe", "dp", "mp", None), P("pipe", "dp", "mp", None), P("pipe", "dp", "mp"), P(None, "dp", None),
        P("pipe", None, None), P("pipe", None, None), P("pipe", "dp", None, "mp"), P("pipe", "mp", "dp"),
        P("pipe", "dp", None, "mp"), P("pipe", "dp", "mp"), P("pipe", None), P("pipe", "mp", "dp"),
        P("pipe", None), P("pipe", None), P("pipe"),
    )
    out = (
        P("pipe", "dp", "mp", None), P("pipe", "dp", "mp", None), P("pipe", None, None), P("pipe", None, None),
        P("pipe", "dp", None, "mp"), P("pipe", "mp", "dp"), P("pipe", "dp", None, "mp"), P("pipe", "dp", "mp"),
        P("pipe", None), P("pipe", "mp", "dp"), P("pipe", None), P("pipe", None), P("pipe"), P("pipe", None),
    )
    return jax.shard_map(on_device, mesh=mesh, in_specs=split, out_specs=out, check_vma=False)
```

time: 2310 us -> 116 us (0.05)
  waiting for transfers between devices: 1330 us -> 0 us
  blocking collectives: 702 us -> 0 us
  Pallas kernels: 0 us -> 114 us
  matrix products: 102 us -> 0 us
  other arithmetic: 78.6 us -> 0 us
  local copies, waits for them, and re-layouts: 48.5 us -> 0 us
    reduce_scatter x30 -> x0, waiting for transfers between devices: 1190 us -> none  [the longest x3 223 us: spread(): lax.psum_scatter(g_in.astype(jnp.bfloat16), 'dp', scatter_dimension=0, ti...]
    all_gather x23 -> x0, blocking collectives: 355 us -> none  [the longest x9 117 us: rows_in(): return lax.all_gather(value, 'mp', axis=0, tiled=True)]
    psum x1 -> x0, blocking collectives: 347 us -> none  [on_device(): lax.psum((small_sum[0], small_sum[1], small_sum[2], small_sum[3], small_s...]
    pallas_call x0 -> x2, Pallas kernels: none -> 114 us  [the longest x1 112 us: on_device(): pl.pallas_call(kernel, out_shape=[jax.ShapeDtypeStruct((2, 128, T), BF),...]
    dot_general x66 -> x0, matrix products: 101 us -> none  [the longest x3 12.9 us: one_block(): jnp.einsum('hqk,khd->qhd', d_scores, key_rows, preferred_element_type=jnp...]
    unnamed x36 -> x0, waiting for transfers between devices: 79.2 us -> none
    ppermute x6 -> x0, waiting for transfers between devices: 60.1 us -> none  [passed_along(): lax.ppermute(value, axis, [(source, source + steps) for source in range(l...]
    reduce_sum x32 -> x0, other arithmetic: 33.3 us -> none  [the longest x8 14.1 us: norm_back(): jnp.sum(grad * unit, 0)]
  transfers between devices with their start and end apart: 39 -> 0, of which waited for: 36 -> 0; matrix products, arithmetic and copies ran while one was open for 6% -> 0% of each run, Pallas kernels for 0% -> 0%
where the time goes in v1:
time: 116 us
  Pallas kernels  114 us (98%)
  between operations  1.46 us (1%)
    pallas_call x1, Pallas kernels, on_device(): pl.pallas_call(kernel, out_shape=[jax.ShapeDtypeStruct((2, 128, T), BF),...  112 us

profile of v1, /device:TPU:0, one launch (start us, length us, event | category | flops | bytes accessed | tf_op | source)
XLA Modules:
  0.0 115.8 jit_solution(15407441388747478187)
XLA Ops:
  1.3 112.1 %step.1 = (bf16[2,128,512]{2,1,0:T(8,128)(2,1)}, bf16[2,128,512]{2,1,0:T(8,128)(2,1)}, bf16[2,32,512]{2,1,0:T(8,128)(2,1)}, bf16[2,32,1024]{2,1,0:T(8,128)(2,1)}...) custom-call(bf16[2,128,512]{2,1,0:T(8,128)(2,1)} %bitcast.35, bf16[2,128,512]{2,1,0:T(8,128)(2,1)} %bitcast.36, ...), custom_call_target="tpu_custom_call" | custom-call | tf_op jit(solution)/shard_map/step/pallas_call | solution.py:913
  113.4 2.2 %finish.1 = (bf16[2,128,512]{2,1,0:T(8,128)(2,1)}, f32[2,128,512]{2,1,0:T(8,128)}, f32[3,1,512]{2,1,0:T(1,128)}, f32[3,1,512]{2,1,0:T(1,128)}, f32[3,32,128]{2,1...) custom-call(bf16[2,128,512]{2,1,0:T(8,128)(2,1)} %get-tuple-element., ...), custom_call_target="tpu_custom_call" | custom-call | tf_op jit(solution)/shard_map/finish/pallas_call | solution.py:934

commit v2 on v1

--- a/solution.py
+++ b/solution.py
@@ -34,7 +34,6 @@
     U=((3, T, T), F32),
     F=((3, T, 128), F32),
     N=((3, T, T), BF),
-    NT=((3, T, T), BF),
     QKV=((2, T, 384), BF),
     KT=((2, 128, T), BF),
     VT=((2, 128, T), BF),
@@ -55,13 +54,11 @@
     DX=((T, T), F32),
     FF=((T, T), BF),
     FB=((T, T), BF),
-    LT=((T, T), BF),
     XS=((3, T, T), BF),
     XR=((3, T, T), BF),
     BS=((T, T), F32),
     BX=((T, T), F32),
     MEM=((T, T), BF),
-    MT=((T, T), BF),
     DM=((T, T), BF),
     DS=((T, T), BF),
     DSR=((T, T), BF),
@@ -75,16 +72,17 @@
     G0=((2, 4, 4, 32, 512), BF),
     G1=((2, 4, 4, 32, 1024), BF),
     G2=((2, 4, 4, 32, 512), BF),
-    LA0=((2, 3, 4, 32, 512), BF),
-    LA1=((2, 3, 4, 32, 1024), BF),
-    LA2=((2, 3, 4, 32, 512), BF),
+    RX0=((2, 2, 2, 32, 512), BF),
+    RF0=((2, 2, 4, 32, 512), BF),
+    RX1=((2, 2, 2, 32, 1024), BF),
+    RF1=((2, 2, 4, 32, 1024), BF),
+    RX2=((2, 2, 2, 32, 512), BF),
+    RF2=((2, 2, 4, 32, 512), BF),
     SA0=((2, 4, 32, 512), BF),
     SA1=((2, 4, 32, 1024), BF),
     SA2=((2, 4, 32, 512), BF),
-    LB0=((2, 3, 32, 512), BF),
     LB1=((2, 3, 32, 1024), BF),
     LB2=((2, 3, 32, 512), BF),
-    SB0=((2, 32, 512), BF),
     SB1=((2, 32, 1024), BF),
     SB2=((2, 32, 512), BF),
     SM=((SMALL, T), F32),
@@ -105,15 +103,17 @@
     hl=(4,),
     ct=(4,),
     lo=(6,),
-    ga=(3, 2, 2, 3),
-    ex=(3, 4),
+    ga=(3, 3, 2, 3),
+    ex=(3, 2),
     mem=(4, 2),
     mfw=(4,),
     dmx=(4,),
     dme=(4, 2),
     dmf=(4,),
-    rs=(3, 2, 2, 3),
+    rs=(3, 2, 2, 6),
+    rt=(3, 2, 3),
     rc=(3, 2),
+    r0=(2, 4),
     os=(2,),
     od=(2,),
     m1=(3,),
@@ -166,8 +166,8 @@
     for k, name in enumerate(SEMS):
         ss[name], rs[name] = rest[2 * k], rest[2 * k + 1]
     W, G = (r.W0, r.W1, r.W2), (r.G0, r.G1, r.G2)
-    LA, SA = (r.LA0, r.LA1, r.LA2), (r.SA0, r.SA1, r.SA2)
-    LB, SB = (r.LB0, r.LB1, r.LB2), (r.SB0, r.SB1, r.SB2)
+    RX, RF, SA = (r.RX0, r.RX1, r.RX2), (r.RF0, r.RF1, r.RF2), (r.SA0, r.SA1, r.SA2)
+    LB, SB = (None, r.LB1, r.LB2), (None, r.SB1, r.SB2)
     LC = (o_c0, o_c1, o_c2)
 
     c = lax.axis_index("pipe")
@@ -250,6 +250,7 @@
     for d in (1, 2, 3):
         partners.append(dev(core=role, zz=zb[d], xx=2 * c))
         partners.append(dev(core=role, yy=yb[d], xx=2 * c + 1))
+        partners += [dev(core=x // 2, yy=to_y[d], zz=to_z[d], xx=home) for home in (c, 3 - c)]
     for to in partners:
         pl.semaphore_signal(barrier, inc=1, device_id=to, device_id_type=MESH)
 
@@ -283,6 +284,18 @@
             put(lambda d=d: (W[g].at[0, y, z], W[g].at[0, y, z], ss["ga"].at[g, 0, 0, d - 1], rs["ga"].at[g, 0, 0, d - 1], dev(zz=zs[d])), dec if g == 2 else None)
             put(lambda d=d: (W[g].at[1, y, z], W[g].at[1, y, z], ss["ga"].at[g, 0, 1, d - 1], rs["ga"].at[g, 0, 1, d - 1], dev(yy=ys[d])), dec if g == 2 else None)
 
+    low_half, high_half = pl.ds(0, 2), pl.ds(2, 2)
+
+    def block(ref, jj, at, half=None):
+        if jj == 0:
+            return ref.at[0, at] if half is None else ref.at[0, at, half]
+        return ref.at[1, :, at] if half is None else ref.at[1, half, at]
+
+    def along(jj, d):
+        if jj == 0:
+            return ys[d % 4], dev(yy=ys[d % 4])
+        return zs[d % 4], dev(zz=zs[d % 4])
+
     def gather_second(g):
         for d in range(4):
             if g == 0:
@@ -291,47 +304,102 @@
             elif d > 0:
                 got(W[g].at[0, y, zb[d]], rs["ga"].at[g, 0, 0, d - 1])
                 got(W[g].at[1, yb[d], z], rs["ga"].at[g, 0, 1, d - 1])
-        for d in (1, 2, 3):
-            put(lambda d=d: (W[g].at[0, y], W[g].at[0, y], ss["ga"].at[g, 1, 0, d - 1], rs["ga"].at[g, 1, 0, d - 1], dev(yy=ys[d])), dec if g == 2 else None)
-            put(lambda d=d: (W[g].at[1, :, z], W[g].at[1, :, z], ss["ga"].at[g, 1, 1, d - 1], rs["ga"].at[g, 1, 1, d - 1], dev(zz=zs[d])), dec if g == 2 else None)
+        for jj in (0, 1):
+            for k, d in ((0, 1), (1, 3)):
+                def what(jj=jj, k=k, d=d):
+                    mine = block(W[g], jj, along(jj, 0)[0])
+                    return mine, mine, ss["ga"].at[g, 1, jj, k], rs["ga"].at[g, 1, jj, k], along(jj, d)[1]
+
+                put(what, dec if g == 2 else None)
+
+    def gather_pass(g):
+        for jj in (0, 1):
+            for k, d in ((0, 1), (1, 3)):
+                behind = along(jj, 4 - d)[0]
+                got(block(W[g], jj, behind), rs["ga"].at[g, 1, jj, k])
+
+                def what(jj=jj, k=k, d=d):
+                    part = block(W[g], jj, along(jj, 4 - d)[0], (low_half, high_half)[k])
+                    return part, part, ss["ga"].at[g, 2, jj, k], rs["ga"].at[g, 2, jj, k], along(jj, d)[1]
+
+                put(what, dec if g == 2 else None)
 
     def gather_done(g):
-        for d in (1, 2, 3):
-            got(W[g].at[0, yb[d]], rs["ga"].at[g, 1, 0, d - 1])
-            got(W[g].at[1, :, zb[d]], rs["ga"].at[g, 1, 1, d - 1])
-
-    def reduce_first(g, jj, when=None):
-        for d in (1, 2, 3):
-            def what(d=d):
-                src, to = (G[g].at[0, ys[d]], dev(yy=ys[d])) if jj == 0 else (G[g].at[1, :, zs[d]], dev(zz=zs[d]))
-                return src, LA[g].at[jj, d - 1], ss["rs"].at[g, 0, jj, d - 1], rs["rs"].at[g, 0, jj, d - 1], to
-
-            put(what, when)
+        for jj in (0, 1):
+            for k in (0, 1):
+                got(block(W[g], jj, along(jj, 2)[0], (low_half, high_half)[k]), rs["ga"].at[g, 2, jj, k])
+
+    def reduce_first(g, jj, h=0, when=None):
+        cols = pl.ds(512 * h, 512)
+        for k, d in ((0, 1), (1, 3)):
+            halves = (low_half, high_half)
+
+            def far(k=k, d=d):
+                return (block(G[g].at[..., cols], jj, along(jj, 2)[0], halves[k]), RX[g].at[jj, k, :, :, cols],
+                        ss["rs"].at[g, h, jj, k], rs["rs"].at[g, h, jj, k], along(jj, d)[1])
+
+            put(far, when)
+        for k, d in ((0, 1), (1, 3)):
+            def near(k=k, d=d):
+                return (block(G[g].at[..., cols], jj, along(jj, d)[0], halves[1 - k]),
+                        RF[g].at[jj, k, halves[1 - k], :, cols],
+                        ss["rs"].at[g, h, jj, 2 + k], rs["rs"].at[g, h, jj, 2 + k], along(jj, d)[1])
+
+            put(near, when)
+
+    def reduce_pass(g, h=0, when=None):
+        cols = pl.ds(512 * h, 512)
+        for jj in (0, 1):
+            for k, d in ((0, 1), (1, 3)):
+                got(RX[g].at[jj, k, :, :, cols], rs["rs"].at[g, h, jj, k])
+                at = along(jj, d)[0]
+                own = G[g][0, at, 2 * k:2 * k + 2, :, cols] if jj == 0 else G[g][1, 2 * k:2 * k + 2, at, :, cols]
+                RX[g][jj, k, :, :, cols] = (own.astype(F32) + RX[g][jj, k, :, :, cols].astype(F32)).astype(BF)
+
+                def what(jj=jj, k=k, d=d):
+                    return (RX[g].at[jj, k, :, :, cols], RF[g].at[jj, k, (low_half, high_half)[k], :, cols],
+                            ss["rs"].at[g, h, jj, 4 + k], rs["rs"].at[g, h, jj, 4 + k], along(jj, d)[1])
+
+                put(what, when)
 
     def reduce_second(g):
         for jj in (0, 1):
+            for k in (0, 1):
+                for h in (0, 1) if g == 1 else (0,):
+                    cols = pl.ds(512 * h, 512)
+                    halves = (low_half, high_half)
+                    got(RF[g].at[jj, k, halves[1 - k], :, cols], rs["rs"].at[g, h, jj, 2 + k])
+                    got(RF[g].at[jj, k, halves[k], :, cols], rs["rs"].at[g, h, jj, 4 + k])
+
+            def add(i):
+                own = G[g][0, y, i] if jj == 0 else G[g][1, i, z]
+                total = own.astype(F32) + RF[g][jj, 0, i].astype(F32) + RF[g][jj, 1, i].astype(F32)
+                SA[g][jj, i] = total.astype(BF)
+
+            loop(4, add)
+            if g == 0:
+                put_or_keep(lambda jj=jj: (
+                    SA[0].at[jj, z if jj == 0 else y], o_c0.at[m, 0], ss["r0"].at[jj, 0], rs["r0"].at[m, 0],
+                    role, 2 * c + jj))
+                for d in (1, 2, 3):
+                    put(lambda jj=jj, d=d: (
+                        SA[0].at[jj, zs[d] if jj == 0 else ys[d]], o_c0.at[m, d], ss["r0"].at[jj, d],
+                        rs["r0"].at[m, d],
+                        dev(core=role, zz=zs[d], xx=2 * c) if jj == 0 else dev(core=role, yy=ys[d], xx=2 * c + 1)))
+            else:
+                for d in (1, 2, 3):
+                    def what(d=d, jj=jj):
+                        src, to = ((SA[g].at[0, zs[d]], dev(zz=zs[d])) if jj == 0 else
+                                   (SA[g].at[1, ys[d]], dev(yy=ys[d])))
+                        return (src, LB[g].at[jj, d - 1], ss["rt"].at[g, jj, d - 1],
+                                rs["rt"].at[g, jj, d - 1], to)
+
+                    put(what, dec if g == 2 else None)
+
+    def reduce_third(g):
+        for jj in (0, 1):
             for d in (1, 2, 3):
-                got(LA[g].at[jj, d - 1], rs["rs"].at[g, 0, jj, d - 1])
-
-            def add(k):
-                own = G[g][0, y, k] if jj == 0 else G[g][1, k, z]
-                total = own.astype(F32)
-                for d in range(3):
-                    total = total + LA[g][jj, d, k].astype(F32)
-                SA[g][jj, k] = total.astype(BF)
-
-            loop(4, add)
-            for d in (1, 2, 3):
-                def what(d=d, jj=jj):
-                    src, to = (SA[g].at[0, zs[d]], dev(zz=zs[d])) if jj == 0 else (SA[g].at[1, ys[d]], dev(yy=ys[d]))
-                    return src, LB[g].at[jj, d - 1], ss["rs"].at[g, 1, jj, d - 1], rs["rs"].at[g, 1, jj, d - 1], to
-
-                put(what, dec if g == 2 else None)
-
-    def reduce_third(g):
-        for jj in (0, 1):
-            for d in (1, 2, 3):
-                got(LB[g].at[jj, d - 1], rs["rs"].at[g, 1, jj, d - 1])
+                got(LB[g].at[jj, d - 1], rs["rt"].at[g, jj, d - 1])
             total = (SA[g][0, z] if jj == 0 else SA[g][1, y]).astype(F32)
             for d in range(3):
                 total = total + LB[g][jj, d].astype(F32)
@@ -346,7 +414,7 @@
                     SB[g].at[jj], LC[g].at[m], ss["rc"].at[g, jj], rs["rc"].at[g, m], role, 2 * c + jj))
 
     def half_rows(i, core):
-        return pl.ds(pl.multiple_of(128 * i + 64 * core, 64), 64)
+        return pl.ds(pl.multiple_of(256 * (i // 2) + 128 * core + 64 * lax.rem(i, 2), 64), 64)
 
     def memory_copy(i):
         part = half_rows(i, c)
@@ -369,7 +437,7 @@
         return rdma(r.DM.at[part], r.DM.at[part], ss["dmf"].at[i], rs["dme"].at[i, c], dev(core=sib))
 
     def exchange_copy(k, i):
-        part = rows_of(i, 128)
+        part = rows_of(i, 256)
         return rdma(r.XS.at[k, part], r.XR.at[k, part], ss["ex"].at[k, i], rs["ex"].at[k, i], dev(core=sib))
 
     for d in range(4):
@@ -401,6 +469,7 @@
             r.PCB, r.W2.at[jj_me, y, z, :, pl.ds(pl.multiple_of(256 * c, 256), 256)], ss["po"].at[k],
             rs["pc"].at[jj_me, c], x // 2, k + 1))
     gather_second(1)
+    gather_pass(0)
     for k in (0, 1):
         for core in (0, 1):
             put_or_keep(lambda k=k, core=core: (
@@ -439,20 +508,16 @@
     def both(g, lo, hi):
         return jnp.concatenate([weight(g, 0, lo, hi), weight(g, 1, lo, hi)], axis=1)
 
-    def send_part(k, i, size, value):
-        r.XS[k, rows_of(i, size)] = value.astype(BF)
-        for h in range(size // 128):
-            exchange_copy(k, i * (size // 128) + h).start()
+    def send_part(k, i, value):
+        r.XS[k, rows_of(i, 256)] = value.astype(BF)
+        exchange_copy(k, i).start()
 
     def received(k, part):
         return r.XS[k, part].astype(F32) + r.XR[k, part].astype(F32)
 
     def after_exchange(k, i, body):
-        def one(h):
-            exchange_copy(k, 2 * i + h).wait()
-            body(rows_of(2 * i + h, 128))
-
-        loop(2, one)
+        exchange_copy(k, i).wait()
+        body(rows_of(i, 256))
 
     low_lane = lax.broadcasted_iota(jnp.int32, (1, 128), 1) < 64
 
@@ -486,29 +551,19 @@
             r.DQ[jj, :, dv_at:dv_at + 128] = jnp.where(low_lane, dvs[0], dvs[1]).astype(BF)
             r.DQ[jj, :, dq_at:dq_at + 128] = (jnp.concatenate(dqs, axis=0).T * SCALE).astype(BF)
 
-    def flip(target, source):
-        def one(i):
-            part = rows_of(i, 128)
-            target[part, :] = source[:, part].T
-
-        loop(4, one)
-
-    def outer(g, jj, lo, hi, left_t, right):
-        def one(h):
-            total = mm(left_t[rows_of(h, 256), :], right())
-            G[g][jj, pl.ds(2 * h, 2), :, :, lo:hi] = total.astype(BF).reshape(2, 4, 32, hi - lo)
-
-        loop(2, one)
+    def outer(g, jj, lo, hi, left, right):
+        G[g][jj, :, :, :, lo:hi] = mm_tn(left[...], right()).astype(BF).reshape(4, 4, 32, hi - lo)
 
     def first(i):
-        part = rows_of(i, 128)
+        part = rows_of(i, 256)
         v = r.IN[part].astype(F32)
-        ln_to(0, part, 128, v)
+        ln_to(0, part, 256, v)
         logit = jnp.sum(v * param(HALTW), axis=-1, keepdims=True) + param(SCAL)[:, 0:1]
-        r.PR[part] = jnp.broadcast_to(jax.nn.sigmoid(logit), (128, 128))
-        r.RN[part] = mm_tn(r.HL[i], jnp.full((16, 128), 1.0 / 16.0, BF))
-
-    loop(4, first)
+        r.PR[part] = jnp.broadcast_to(jax.nn.sigmoid(logit), (256, 128))
+        for h in (0, 1):
+            r.RN[rows_of(2 * i + h, 128)] = mm_tn(r.HL[2 * i + h], jnp.full((16, 128), 1.0 / 16.0, BF))
+
+    loop(2, first)
 
     docs = lax.broadcasted_iota(jnp.int32, (16, T), 0)
     seg_src, seg_tgt = seg[0, pl.ds(m, 1), :], seg[1, pl.ds(m, 1), :]
@@ -535,16 +590,13 @@
     gather_done(0)
 
     for jj in (0, 1):
-        def project(i):
-            part = rows_of(i, 256)
-            three = mm(r.N[0, part], weight(0, jj, 0, 384))
-            r.QKV[jj, part, 0:128] = (three[:, 0:128] * SCALE).astype(BF)
-            r.QKV[jj, part, 128:384] = three[:, 128:384].astype(BF)
-            r.KT[jj, :, part] = three[:, 128:256].T.astype(BF)
-            r.VT[jj, :, part] = three[:, 256:384].T.astype(BF)
-
-        loop(2, project)
-
+        three = mm(r.N[0], weight(0, jj, 0, 384))
+        r.QKV[jj, :, 0:128] = (three[:, 0:128] * SCALE).astype(BF)
+        r.QKV[jj, :, 128:384] = three[:, 128:384].astype(BF)
+        r.KT[jj] = three[:, 128:256].T.astype(BF)
+        r.VT[jj] = three[:, 256:384].T.astype(BF)
+
+    gather_pass(1)
     attend(lambda jj: r.QKV[jj, :, 0:128], r.QKV, 128, r.VT, r.BS, r.PA, r.HD)
 
     @pl.when(dec)
@@ -554,7 +606,7 @@
     def self_out(i):
         part = rows_of(i, 256)
         heads = jnp.concatenate([r.HD[0, part], r.HD[1, part]], axis=1)
-        send_part(0, i, 256, mm_nt(heads, both(0, 384, 512)))
+        send_part(0, i, mm_nt(heads, both(0, 384, 512)))
 
     loop(2, self_out)
     second = jnp.where(enc, 2, 1)
@@ -562,10 +614,11 @@
     def self_after(part):
         v = r.IN[part].astype(F32) + received(0, part)
         r.AS[part] = v
-        ln_to(second, part, 128, v)
+        ln_to(second, part, 256, v)
 
     @pl.when(dec)
     def _():
+        gather_pass(2)
         gather_done(2)
         loop(2, lambda i: after_exchange(0, i, self_after))
         for jj in (0, 1):
@@ -574,32 +627,27 @@
                 r.CQ[jj, part] = (mm(r.N[1, part], weight(2, jj, 256, 384)) * SCALE).astype(BF)
 
             loop(2, ask)
-        flip(r.NT.at[0], r.N.at[0])
 
         def memory_in(i):
-            @pl.when(i < 4)
-            def _():
-                got(r.MEM.at[half_rows(i, c)], rs["mem"].at[i, c])
-                memory_forward(i).start()
-
-            @pl.when(i > 0)
-            def _():
-                j = i - 1
-                got(r.MEM.at[half_rows(j, sib)], rs["mem"].at[j, sib])
-                part = rows_of(j, 128)
-                for jj in (0, 1):
-                    pairs = mm(r.MEM[part], weight(2, jj, 0, 256))
-                    r.CKV[jj, part] = pairs.astype(BF)
-                    r.CKT[jj, :, part] = pairs[:, 0:128].T.astype(BF)
-                    r.CVT[jj, :, part] = pairs[:, 128:256].T.astype(BF)
-
-        loop(5, memory_in)
+            for p in (0, 1):
+                got(r.MEM.at[half_rows(2 * i + p, c)], rs["mem"].at[2 * i + p, c])
+                memory_forward(2 * i + p).start()
+            for p in (0, 1):
+                got(r.MEM.at[half_rows(2 * i + p, sib)], rs["mem"].at[2 * i + p, sib])
+            part = rows_of(i, 256)
+            for jj in (0, 1):
+                pairs = mm(r.MEM[part], weight(2, jj, 0, 256))
+                r.CKV[jj, part] = pairs.astype(BF)
+                r.CKT[jj, :, part] = pairs[:, 0:128].T.astype(BF)
+                r.CVT[jj, :, part] = pairs[:, 128:256].T.astype(BF)
+
+        loop(2, memory_in)
         attend(lambda jj: r.CQ[jj], r.CKV, 0, r.CVT, r.BX, r.PX, r.HX)
 
         def cross_out(i):
             part = rows_of(i, 256)
             heads = jnp.concatenate([r.HX[0, part], r.HX[1, part]], axis=1)
-            send_part(2, i, 256, mm_nt(heads, both(2, 384, 512)))
+            send_part(2, i, mm_nt(heads, both(2, 384, 512)))
 
         loop(2, cross_out)
 
@@ -608,7 +656,7 @@
     def cross_after(part):
         v = r.AS[part] + received(2, part)
         r.AS[part] = v
-        ln_to(2, part, 128, v)
+        ln_to(2, part, 256, v)
 
     def ffn(i):
         pl.when(enc)(lambda: after_exchange(0, i, self_after))
@@ -626,7 +674,7 @@
             r.ACT[jj, part] = act
             term = mm_nt(act, weight(1, jj, 512, 1024))
             total = term if total is None else total + term
-        send_part(1, i, 256, total)
+        send_part(1, i, total)
 
     loop(2, ffn)
 
@@ -648,11 +696,12 @@
     def _():
         def memory_out(i):
             exchange_copy(1, i).wait()
-            part = rows_of(i, 128)
-            ln_to(1, part, 128, ffn_after(part))
-            memory_copy(i).start()
-
-        loop(4, memory_out)
+            part = rows_of(i, 256)
+            ln_to(1, part, 256, ffn_after(part))
+            for p in (0, 1):
+                memory_copy(2 * i + p).start()
+
+        loop(2, memory_out)
         r.OB[...] = r.N[1]
 
     for q in range(4):
@@ -681,33 +730,36 @@
             memory_grad_forward(2 * i + h).start()
 
     def memory_grad_in(i):
-        def one(h):
-            j = 2 * i + h
-            got(r.DM.at[half_rows(j, sib)], rs["dme"].at[j, sib])
-            part = rows_of(j, 128)
-            n = r.COT[part].astype(F32) + r.DM[part].astype(F32)
-            halt_back(part, ln_back(1, part, n))
-
-        loop(2, one)
+        for h in (0, 1):
+            got(r.DM.at[half_rows(2 * i + h, sib)], rs["dme"].at[2 * i + h, sib])
+        part = rows_of(i, 256)
+        n = r.COT[part].astype(F32) + r.DM[part].astype(F32)
+        halt_back(part, ln_back(1, part, n))
         pl.when(i == 0)(lambda: memory_grad_pass(1))
 
     def output_in(i):
-        def one(h):
-            exchange_copy(1, 2 * i + h).wait()
-            part = rows_of(2 * i + h, 128)
-            r.OB[part] = ffn_after(part).astype(BF)
-            halt_back(part, r.COT[part].astype(F32))
-
-        loop(2, one)
+        exchange_copy(1, i).wait()
+        part = rows_of(i, 256)
+        r.OB[part] = ffn_after(part).astype(BF)
+        halt_back(part, r.COT[part].astype(F32))
+
+    def down_weights():
+        for jj in (0, 1):
+            outer(1, jj, 512, 1024, r.FF, lambda: r.ACT[jj])
+
+    def up_weights():
+        for jj in (0, 1):
+            outer(1, jj, 0, 512, r.N.at[2], lambda: r.PB[jj])
 
     @pl.when(enc)
     def _():
-        flip(r.NT.at[2], r.N.at[2])
-        flip(r.NT.at[0], r.N.at[0])
         memory_grad_pass(0)
+        loop(2, memory_grad_in)
+        down_weights()
+        for jj in (0, 1):
+            reduce_first(1, jj, 1, enc)
 
     def ffn_back(i):
-        pl.when(enc)(lambda: memory_grad_in(i))
         pl.when(dec)(lambda: output_in(i))
         part = rows_of(i, 256)
         total = None
@@ -719,7 +771,7 @@
             r.PB[jj, part] = low
             term = mm_nt(low, weight(1, jj, 0, 512))
             total = term if total is None else total + term
-        send_part(0, i, 256, total)
+        send_part(0, i, total)
 
     loop(2, ffn_back)
     for h in (0, 1):
@@ -727,14 +779,12 @@
         put_or_keep(lambda h=h, quarter=quarter: (
             r.OB.at[rows_of(quarter, 128)], o_st.at[m], ss["os"].at[h], rs["os"].at[m], role, quarter))
 
-    def ffn_weights(when):
-        flip(r.LT, r.FF)
-        for jj in (0, 1):
-            outer(1, jj, 0, 512, r.NT.at[2], lambda: r.PB[jj])
-            outer(1, jj, 512, 1024, r.LT, lambda: r.ACT[jj])
-            reduce_first(1, jj, when)
-
-    pl.when(enc)(lambda: ffn_weights(enc))
+    @pl.when(enc)
+    def _():
+        up_weights()
+        for jj in (0, 1):
+            reduce_first(1, jj, 0, enc)
+        reduce_pass(1, 1, enc)
 
     def ffn_back_after(part):
         d = r.DA[part] + ln_back(2, part, received(0, part))
@@ -758,12 +808,13 @@
         attend_back(lambda jj: r.CQ[jj], r.CKV, 128, r.CKT, r.PX, 256, 0, 128)
 
         def memory_back(i):
-            part = rows_of(i, 128)
+            part = rows_of(i, 256)
             pairs = jnp.concatenate([r.DQ[0, part, 0:256], r.DQ[1, part, 0:256]], axis=1)
             r.DS[part] = mm_nt(pairs, both(2, 0, 256)).astype(BF)
-            memory_grad_swap(i).start()
-
-        loop(4, memory_back)
+            for p in (0, 1):
+                memory_grad_swap(2 * i + p).start()
+
+        loop(2, memory_back)
 
         def memory_grad_out(i):
             part = half_rows(i, c)
@@ -772,50 +823,57 @@
             memory_grad_copy(i).start()
 
         loop(4, memory_grad_out)
-        flip(r.NT.at[2], r.N.at[2])
-        ffn_weights(dec)
+        down_weights()
+        for jj in (0, 1):
+            reduce_first(1, jj, 1, dec)
+        up_weights()
+        for jj in (0, 1):
+            reduce_first(1, jj, 0, dec)
 
         def query_back(i):
             part = rows_of(i, 256)
             asked = jnp.concatenate([r.DQ[0, part, 256:384], r.DQ[1, part, 256:384]], axis=1)
-            send_part(1, i, 256, mm_nt(asked, both(2, 256, 384)))
+            send_part(1, i, mm_nt(asked, both(2, 256, 384)))
 
         loop(2, query_back)
-        flip(r.LT, r.FB)
-        flip(r.NT.at[1], r.N.at[1])
-        flip(r.MT, r.MEM)
-        for jj in (0, 1):
-            outer(2, jj, 0, 256, r.MT, lambda: r.DQ[jj, :, 0:256])
-            outer(2, jj, 256, 384, r.NT.at[1], lambda: r.DQ[jj, :, 256:384])
-            outer(2, jj, 384, 512, r.LT, lambda: r.HX[jj])
-            reduce_first(2, jj, dec)
+        for jj in (0, 1):
+            outer(2, jj, 0, 256, r.MEM, lambda: r.DQ[jj, :, 0:256])
+            outer(2, jj, 256, 384, r.N.at[1], lambda: r.DQ[jj, :, 256:384])
+            outer(2, jj, 384, 512, r.FB, lambda: r.HX[jj])
+            reduce_first(2, jj, 0, dec)
 
         def cross_back_after(part):
             d = r.DA[part] + ln_back(1, part, received(1, part))
             r.DA[part] = d
             r.FB[part] = d.astype(BF)
 
+        reduce_pass(1, 1, dec)
+
         def after_query_back(i):
             after_exchange(1, i, cross_back_after)
             heads_back(0, i)
 
         loop(2, after_query_back)
 
-    flip(r.LT, r.FB)
     for jj in (0, 1):
-        outer(0, jj, 384, 512, r.LT, lambda: r.HD[jj])
+        outer(0, jj, 384, 512, r.FB, lambda: r.HD[jj])
     attend_back(lambda jj: r.QKV[jj, :, 0:128], r.QKV, 256, r.KT, r.PA, 0, 128, 256)
 
+    reduce_pass(1, 0)
     for jj in (0, 1):
-        outer(0, jj, 0, 384, r.NT.at[0], lambda: r.DQ[jj])
+        outer(0, jj, 0, 384, r.N.at[0], lambda: r.DQ[jj])
         reduce_first(0, jj)
 
     def first_back(i):
         part = rows_of(i, 256)
         all_three = jnp.concatenate([r.DQ[0, part], r.DQ[1, part]], axis=1)
-        send_part(2, i, 256, mm_nt(all_three, both(0, 0, 384)))
+        send_part(2, i, mm_nt(all_three, both(0, 0, 384)))
 
     loop(2, first_back)
+
+    @pl.when(dec)
+    def _():
+        reduce_pass(2, 0, dec)
 
     def first_back_after(part):
         d = r.DX[part] + r.DA[part] + ln_back(0, part, received(2, part))
@@ -831,38 +889,40 @@
     r.SM2[...] = jnp.where(jnp.logical_or(halves, c == 0), r.SM[...], 0.0)
     for d in (1, 2, 3):
         put(lambda d=d: (r.SM2, r.LM1.at[d - 1], ss["m1"].at[d - 1], rs["m1"].at[d - 1], dev(zz=zs[d])))
-    reduce_second(1)
-
-    @pl.when(dec)
-    def _():
-        reduce_second(2)
-
+    reduce_pass(0)
     for d in range(3):
         got(r.LM1.at[d], rs["m1"].at[d])
     r.SM3[...] = r.SM2[...] + r.LM1[0] + r.LM1[1] + r.LM1[2]
     for d in (1, 2, 3):
         put(lambda d=d: (r.SM3, r.LM2.at[d - 1], ss["m2"].at[d - 1], rs["m2"].at[d - 1], dev(yy=ys[d])))
 
+    reduce_second(1)
+
+    @pl.when(dec)
+    def _():
+        reduce_second(2)
+
     reduce_second(0)
-    reduce_third(1)
-
-    @pl.when(dec)
-    def _():
-        reduce_third(2)
-
     for d in range(3):
         got(r.LM2.at[d], rs["m2"].at[d])
     r.SM[...] = r.SM3[...] + r.LM2[0] + r.LM2[1] + r.LM2[2]
     for k in range(4):
         put_or_keep(lambda k=k: (r.SM, o_sm.at[2 * m + c], ss["m3"].at[k], rs["m3"].at[2 * m + c], role, k))
-    reduce_third(0)
+    reduce_third(1)
+
+    @pl.when(dec)
+    def _():
+        reduce_third(2)
+
     for k in range(4):
         got(o_sm.at[k], rs["m3"].at[k])
     for k in (0, 1):
         got(o_st.at[k], rs["os"].at[k])
         got(o_dx.at[k], rs["od"].at[k])
-        for g in range(3):
+        for g in (1, 2):
             got(LC[g].at[k], rs["rc"].at[g, k])
+        for d in range(4):
+            got(o_c0.at[k, d], rs["r0"].at[k, d])
 
     @pl.when(enc)
     def _():
@@ -885,7 +945,9 @@
            o_haltw, o_haltb, o_act):
     o_st[...] = st[...]
     o_dx[...] = dx[...].astype(F32)
-    both = c0[0].astype(F32) + c0[1].astype(F32)
+    both = c0[0, 0].astype(F32)
+    for k in range(1, 8):
+        both = both + c0[k // 4, k % 4].astype(F32)
     for k in range(3):
         o_in[k] = both[:, 128 * k:128 * k + 128]
     o_out[...] = both[:, 384:512]
@@ -915,7 +977,7 @@
         out_shape=[
             jax.ShapeDtypeStruct((2, 128, T), BF),
             jax.ShapeDtypeStruct((2, 128, T), BF),
-            jax.ShapeDtypeStruct((2, 32, 512), BF),
+            jax.ShapeDtypeStruct((2, 4, 32, 512), BF),
             jax.ShapeDtypeStruct((2, 32, 1024), BF),
             jax.ShapeDtypeStruct((2, 32, 256), BF),
             jax.ShapeDtypeStruct((4, SMALL, T), F32),

time: 116 us -> 112 us (0.966); the launches traced: 116 us -> 111 us
  Pallas kernels: 114 us -> 109 us
    pallas_call x1, Pallas kernels: 112 us -> 107 us  [on_device(): pl.pallas_call(kernel, out_shape=[jax.ShapeDtypeStruct((2, 128, T), BF),...]
where the time goes in v2:
time: 112 us; the launch traced here: 111 us
  Pallas kernels  109 us (97%)
  between operations  1.48 us (1%)
    pallas_call x1, Pallas kernels, on_device(): pl.pallas_call(kernel, out_shape=[jax.ShapeDtypeStruct((2, 128, T), BF),...  107 us
    pallas_call x1, Pallas kernels, on_device(): pl.pallas_call(finish, out_shape=[jax.ShapeDtypeStruct((2, 128, T), BF),...  2.3 us

profile of v2, /device:TPU:0, one launch (start us, length us, event | category | flops | bytes accessed | tf_op | source)
XLA Modules:
  0.0 110.6 jit_solution(17436662311086895653)
XLA Ops:
  1.3 106.8 %step.1 = (bf16[2,128,512]{2,1,0:T(8,128)(2,1)}, bf16[2,128,512]{2,1,0:T(8,128)(2,1)}, bf16[2,4,32,512]{3,2,1,0:T(8,128)(2,1)}, bf16[2,32,1024]{2,1,0:T(8,128)(2...) custom-call(bf16[2,128,512]{2,1,0:T(8,128)(2,1)} %bitcast.35, bf16[2,128,512]{2,1,0:T(8,128)(2,1)} %bitcast.36, ...), custom_call_target="tpu_custom_call" | custom-call | tf_op jit(solution)/shard_map/step/pallas_call | solution.py:975
  108.1 2.3 %finish.1 = (bf16[2,128,512]{2,1,0:T(8,128)(2,1)}, f32[2,128,512]{2,1,0:T(8,128)}, f32[3,1,512]{2,1,0:T(1,128)}, f32[3,1,512]{2,1,0:T(1,128)}, f32[3,32,128]{2,1...) custom-call(bf16[2,128,512]{2,1,0:T(8,128)(2,1)} %get-tuple-element., ...), custom_call_target="tpu_custom_call" | custom-call | tf_op jit(solution)/shard_map/finish/pallas_call | solution.py:996

commit v3 on v2

--- a/solution.py
+++ b/solution.py
@@ -56,6 +56,8 @@
     FB=((T, T), BF),
     XS=((3, T, T), BF),
     XR=((3, T, T), BF),
+    XO=((3, T, T), F32),
+    DSF=((T, T), F32),
     BS=((T, T), F32),
     BX=((T, T), F32),
     MEM=((T, T), BF),
@@ -65,15 +67,14 @@
     DSO=((T, T), BF),
     DQ=((2, T, 384), BF),
     DH=((2, T, 128), BF),
-    DSB=((2, T, T), BF),
+    DSB=((2, 2, T, T), BF),
     PR=((T, 128), F32),
     OB=((T, T), BF),
     DXB=((T, T), BF),
     G0=((2, 4, 4, 32, 512), BF),
     G1=((2, 4, 4, 32, 1024), BF),
     G2=((2, 4, 4, 32, 512), BF),
-    RX0=((2, 2, 2, 32, 512), BF),
-    RF0=((2, 2, 4, 32, 512), BF),
+    LA0=((2, 3, 4, 32, 512), BF),
     RX1=((2, 2, 2, 32, 1024), BF),
     RF1=((2, 2, 4, 32, 1024), BF),
     RX2=((2, 2, 2, 32, 512), BF),
@@ -81,15 +82,18 @@
     SA0=((2, 4, 32, 512), BF),
     SA1=((2, 4, 32, 1024), BF),
     SA2=((2, 4, 32, 512), BF),
+    LB0=((2, 3, 32, 512), BF),
     LB1=((2, 3, 32, 1024), BF),
     LB2=((2, 3, 32, 512), BF),
+    SB0=((2, 32, 512), BF),
     SB1=((2, 32, 1024), BF),
     SB2=((2, 32, 512), BF),
     SM=((SMALL, T), F32),
-    LM1=((3, SMALL, T), F32),
-    SM2=((SMALL, T), F32),
-    LM2=((3, SMALL, T), F32),
-    SM3=((SMALL, T), F32),
+    LM1=((3, 8, T), F32),
+    SM2=((8, T), F32),
+    LM2=((3, 8, T), F32),
+    SM3=((8, T), F32),
+    SM4=((8, T), F32),
 )
 
 SEMS = dict(
@@ -103,7 +107,7 @@
     hl=(4,),
     ct=(4,),
     lo=(6,),
-    ga=(3, 3, 2, 3),
+    ga=(4, 3, 2, 3),
     ex=(3, 2),
     mem=(4, 2),
     mfw=(4,),
@@ -112,6 +116,7 @@
     dmf=(4,),
     rs=(3, 2, 2, 6),
     rt=(3, 2, 3),
+    ra=(3, 2, 3),
     rc=(3, 2),
     r0=(2, 4),
     os=(2,),
@@ -166,8 +171,8 @@
     for k, name in enumerate(SEMS):
         ss[name], rs[name] = rest[2 * k], rest[2 * k + 1]
     W, G = (r.W0, r.W1, r.W2), (r.G0, r.G1, r.G2)
-    RX, RF, SA = (r.RX0, r.RX1, r.RX2), (r.RF0, r.RF1, r.RF2), (r.SA0, r.SA1, r.SA2)
-    LB, SB = (None, r.LB1, r.LB2), (None, r.SB1, r.SB2)
+    RX, RF, SA = (None, r.RX1, r.RX2), (None, r.RF1, r.RF2), (r.SA0, r.SA1, r.SA2)
+    LB, SB = (r.LB0, r.LB1, r.LB2), (r.SB0, r.SB1, r.SB2)
     LC = (o_c0, o_c1, o_c2)
 
     c = lax.axis_index("pipe")
@@ -245,12 +250,6 @@
     partners += [dev(core=sib, xx=lax.rem(x + d, 4)) for d in range(4)]
     partners += [dev(xx=lax.rem(x + d, 4)) for d in (1, 2, 3)]
     jj_me = lax.rem(x, 2)
-    to_y = [jnp.where(jj_me == 0, y, ys[d]) for d in range(4)]
-    to_z = [jnp.where(jj_me == 0, zs[d], z) for d in range(4)]
-    for d in (1, 2, 3):
-        partners.append(dev(core=role, zz=zb[d], xx=2 * c))
-        partners.append(dev(core=role, yy=yb[d], xx=2 * c + 1))
-        partners += [dev(core=x // 2, yy=to_y[d], zz=to_z[d], xx=home) for home in (c, 3 - c)]
     for to in partners:
         pl.semaphore_signal(barrier, inc=1, device_id=to, device_id_type=MESH)
 
@@ -279,10 +278,18 @@
 
     homes = (c, 3 - c)
 
+    def gathered(g):
+        return r.W1.at[..., pl.ds(512 * (g // 2), 512)] if g in (1, 3) else W[g]
+
     def gather_first(g):
         for d in (1, 2, 3):
-            put(lambda d=d: (W[g].at[0, y, z], W[g].at[0, y, z], ss["ga"].at[g, 0, 0, d - 1], rs["ga"].at[g, 0, 0, d - 1], dev(zz=zs[d])), dec if g == 2 else None)
-            put(lambda d=d: (W[g].at[1, y, z], W[g].at[1, y, z], ss["ga"].at[g, 0, 1, d - 1], rs["ga"].at[g, 0, 1, d - 1], dev(yy=ys[d])), dec if g == 2 else None)
+            for jj in (0, 1):
+                def what(d=d, jj=jj):
+                    mine = gathered(g).at[jj, y, z]
+                    return (mine, mine, ss["ga"].at[g, 0, jj, d - 1], rs["ga"].at[g, 0, jj, d - 1],
+                            dev(zz=zs[d]) if jj == 0 else dev(yy=ys[d]))
+
+                put(what, dec if g == 2 else None)
 
     low_half, high_half = pl.ds(0, 2), pl.ds(2, 2)
 
@@ -298,16 +305,13 @@
 
     def gather_second(g):
         for d in range(4):
-            if g == 0:
-                got(W[g].at[0, y, zb[d]], rs["g0"].at[0, d])
-                got(W[g].at[1, yb[d], z], rs["g0"].at[1, d])
-            elif d > 0:
-                got(W[g].at[0, y, zb[d]], rs["ga"].at[g, 0, 0, d - 1])
-                got(W[g].at[1, yb[d], z], rs["ga"].at[g, 0, 1, d - 1])
+            if d > 0:
+                got(gathered(g).at[0, y, zb[d]], rs["ga"].at[g, 0, 0, d - 1])
+                got(gathered(g).at[1, yb[d], z], rs["ga"].at[g, 0, 1, d - 1])
         for jj in (0, 1):
             for k, d in ((0, 1), (1, 3)):
                 def what(jj=jj, k=k, d=d):
-                    mine = block(W[g], jj, along(jj, 0)[0])
+                    mine = block(gathered(g), jj, along(jj, 0)[0])
                     return mine, mine, ss["ga"].at[g, 1, jj, k], rs["ga"].at[g, 1, jj, k], along(jj, d)[1]
 
                 put(what, dec if g == 2 else None)
@@ -316,10 +320,10 @@
         for jj in (0, 1):
             for k, d in ((0, 1), (1, 3)):
                 behind = along(jj, 4 - d)[0]
-                got(block(W[g], jj, behind), rs["ga"].at[g, 1, jj, k])
+                got(block(gathered(g), jj, behind), rs["ga"].at[g, 1, jj, k])
 
                 def what(jj=jj, k=k, d=d):
-                    part = block(W[g], jj, along(jj, 4 - d)[0], (low_half, high_half)[k])
+                    part = block(gathered(g), jj, along(jj, 4 - d)[0], (low_half, high_half)[k])
                     return part, part, ss["ga"].at[g, 2, jj, k], rs["ga"].at[g, 2, jj, k], along(jj, d)[1]
 
                 put(what, dec if g == 2 else None)
@@ -327,7 +331,7 @@
     def gather_done(g):
         for jj in (0, 1):
             for k in (0, 1):
-                got(block(W[g], jj, along(jj, 2)[0], (low_half, high_half)[k]), rs["ga"].at[g, 2, jj, k])
+                got(block(gathered(g), jj, along(jj, 2)[0], (low_half, high_half)[k]), rs["ga"].at[g, 2, jj, k])
 
     def reduce_first(g, jj, h=0, when=None):
         cols = pl.ds(512 * h, 512)
@@ -362,9 +366,26 @@
 
                 put(what, when)
 
+    direct_cols = (pl.ds(384, 128), pl.ds(128, 256), pl.ds(0, 128))
+
+    def reduce_direct(e):
+        cols = direct_cols[e]
+        for jj in (0, 1):
+            for d in (1, 2, 3):
+                def what(jj=jj, d=d):
+                    at, to = along(jj, d)
+                    return (block(r.G0.at[..., cols], jj, at), r.LA0.at[jj, d - 1, :, :, cols],
+                            ss["ra"].at[e, jj, d - 1], rs["ra"].at[e, jj, d - 1], to)
+
+                put(what)
+
     def reduce_second(g):
         for jj in (0, 1):
-            for k in (0, 1):
+            if g == 0:
+                for d in range(3):
+                    for e in range(3):
+                        got(r.LA0.at[jj, d, :, :, direct_cols[e]], rs["ra"].at[e, jj, d])
+            for k in (0, 1) if g > 0 else ():
                 for h in (0, 1) if g == 1 else (0,):
                     cols = pl.ds(512 * h, 512)
                     halves = (low_half, high_half)
@@ -373,20 +394,13 @@
 
             def add(i):
                 own = G[g][0, y, i] if jj == 0 else G[g][1, i, z]
-                total = own.astype(F32) + RF[g][jj, 0, i].astype(F32) + RF[g][jj, 1, i].astype(F32)
+                total = own.astype(F32)
+                for k in range(3 if g == 0 else 2):
+                    total = total + (r.LA0 if g == 0 else RF[g])[jj, k, i].astype(F32)
                 SA[g][jj, i] = total.astype(BF)
 
             loop(4, add)
-            if g == 0:
-                put_or_keep(lambda jj=jj: (
-                    SA[0].at[jj, z if jj == 0 else y], o_c0.at[m, 0], ss["r0"].at[jj, 0], rs["r0"].at[m, 0],
-                    role, 2 * c + jj))
-                for d in (1, 2, 3):
-                    put(lambda jj=jj, d=d: (
-                        SA[0].at[jj, zs[d] if jj == 0 else ys[d]], o_c0.at[m, d], ss["r0"].at[jj, d],
-                        rs["r0"].at[m, d],
-                        dev(core=role, zz=zs[d], xx=2 * c) if jj == 0 else dev(core=role, yy=ys[d], xx=2 * c + 1)))
-            else:
+            if True:
                 for d in (1, 2, 3):
                     def what(d=d, jj=jj):
                         src, to = ((SA[g].at[0, zs[d]], dev(zz=zs[d])) if jj == 0 else
@@ -440,23 +454,21 @@
         part = rows_of(i, 256)
         return rdma(r.XS.at[k, part], r.XR.at[k, part], ss["ex"].at[k, i], rs["ex"].at[k, i], dev(core=sib))
 
-    for d in range(4):
-        for k in (0, 1):
-            if d == 0:
-                put_or_keep(lambda k=k: (
-                    r.PSB, r.W0.at[jj_me, y, z], ss["g0"].at[k, 0], rs["g0"].at[jj_me, 0], x // 2, homes[k]))
-            else:
-                put(lambda k=k, d=d: (
-                    r.PSB, r.W0.at[jj_me, y, z], ss["g0"].at[k, d], rs["g0"].at[jj_me, d],
-                    dev(core=x // 2, yy=to_y[d], zz=to_z[d], xx=homes[k])))
+    for k in (0, 1):
+        put_or_keep(lambda k=k: (
+            r.PSB, r.W0.at[jj_me, y, z], ss["g0"].at[k, 0], rs["g0"].at[jj_me, 0], x // 2, homes[k]))
     for k in (0, 1):
         put_or_keep(lambda k=k: (
             r.PFB, r.W1.at[jj_me, y, z], ss["pf"].at[k], rs["pf"].at[jj_me], x // 2, homes[k]))
     put(lambda: (r.PK, r.PSIB, ss["pp"].at[0], rs["pp"].at[0], dev(core=sib)))
     r.SM[...] = jnp.zeros((SMALL, T), F32)
     for jj in (0, 1):
+        got(r.W0.at[jj, y, z], rs["g0"].at[jj, 0])
+    gather_first(0)
+    for jj in (0, 1):
         got(r.W1.at[jj, y, z], rs["pf"].at[jj])
     gather_first(1)
+    gather_first(3)
     for k in (0, 1):
         for core in (0, 1):
             put_or_keep(lambda k=k, core=core: (
@@ -470,6 +482,7 @@
             rs["pc"].at[jj_me, c], x // 2, k + 1))
     gather_second(1)
     gather_pass(0)
+    gather_second(3)
     for k in (0, 1):
         for core in (0, 1):
             put_or_keep(lambda k=k, core=core: (
@@ -509,11 +522,12 @@
         return jnp.concatenate([weight(g, 0, lo, hi), weight(g, 1, lo, hi)], axis=1)
 
     def send_part(k, i, value):
+        r.XO[k, rows_of(i, 256)] = value
         r.XS[k, rows_of(i, 256)] = value.astype(BF)
         exchange_copy(k, i).start()
 
     def received(k, part):
-        return r.XS[k, part].astype(F32) + r.XR[k, part].astype(F32)
+        return r.XO[k, part] + r.XR[k, part].astype(F32)
 
     def after_exchange(k, i, body):
         exchange_copy(k, i).wait()
@@ -536,19 +550,22 @@
                 outs.append(mm(vt[jj, 64 * hh:64 * hh + 64, :], w))
             heads[jj] = jnp.concatenate(outs, axis=0).T.astype(BF)
 
-    def attend_back(q_of, kv, v_at, kt, probs, dq_at, dk_at, dv_at):
+    def attend_back(q_of, kv, v_at, probs, dk_at, dv_at):
         for jj in (0, 1):
             q, o, values = q_of(jj), r.DH[jj], kv[jj, :, v_at:v_at + 128]
             for hh in (0, 1):
                 w = probs[jj, hh].astype(F32)
                 wd = w * mm_nt(values, head_part(o, hh))
                 delta = jnp.sum(wd, axis=0, keepdims=True)
-                r.DSB[hh] = (wd - w * delta).astype(BF)
-            dks = [mm(r.DSB[hh], q) for hh in (0, 1)]
+                r.DSB[jj, hh] = (wd - w * delta).astype(BF)
+            dks = [mm(r.DSB[jj, hh], q) for hh in (0, 1)]
             dvs = [mm(probs[jj, hh], o) for hh in (0, 1)]
-            dqs = [mm(kt[jj, 64 * hh:64 * hh + 64, :], r.DSB[hh]) for hh in (0, 1)]
             r.DQ[jj, :, dk_at:dk_at + 128] = jnp.where(low_lane, dks[0], dks[1]).astype(BF)
             r.DQ[jj, :, dv_at:dv_at + 128] = jnp.where(low_lane, dvs[0], dvs[1]).astype(BF)
+
+    def queries_back(kt, dq_at):
+        for jj in (0, 1):
+            dqs = [mm(kt[jj, 64 * hh:64 * hh + 64, :], r.DSB[jj, hh]) for hh in (0, 1)]
             r.DQ[jj, :, dq_at:dq_at + 128] = (jnp.concatenate(dqs, axis=0).T * SCALE).astype(BF)
 
     def outer(g, jj, lo, hi, left, right):
@@ -587,6 +604,7 @@
                 got(r.W2.at[jj, y, z, :, pl.ds(256 * k, 256)], rs["pc"].at[jj, k])
         gather_first(2)
 
+    gather_pass(1)
     gather_done(0)
 
     for jj in (0, 1):
@@ -596,8 +614,9 @@
         r.KT[jj] = three[:, 128:256].T.astype(BF)
         r.VT[jj] = three[:, 256:384].T.astype(BF)
 
-    gather_pass(1)
     attend(lambda jj: r.QKV[jj, :, 0:128], r.QKV, 128, r.VT, r.BS, r.PA, r.HD)
+
+    gather_pass(3)
 
     @pl.when(dec)
     def _():
@@ -652,6 +671,7 @@
         loop(2, cross_out)
 
     gather_done(1)
+    gather_done(3)
 
     def cross_after(part):
         v = r.AS[part] + received(2, part)
@@ -735,7 +755,6 @@
         part = rows_of(i, 256)
         n = r.COT[part].astype(F32) + r.DM[part].astype(F32)
         halt_back(part, ln_back(1, part, n))
-        pl.when(i == 0)(lambda: memory_grad_pass(1))
 
     def output_in(i):
         exchange_copy(1, i).wait()
@@ -751,16 +770,18 @@
         for jj in (0, 1):
             outer(1, jj, 0, 512, r.N.at[2], lambda: r.PB[jj])
 
-    @pl.when(enc)
-    def _():
-        memory_grad_pass(0)
-        loop(2, memory_grad_in)
-        down_weights()
-        for jj in (0, 1):
-            reduce_first(1, jj, 1, enc)
+    pl.when(enc)(lambda: memory_grad_pass(0))
 
     def ffn_back(i):
+        pl.when(enc)(lambda: memory_grad_in(i))
         pl.when(dec)(lambda: output_in(i))
+
+        @pl.when(jnp.logical_and(enc, i == 1))
+        def _():
+            down_weights()
+            for jj in (0, 1):
+                reduce_first(1, jj, 1, enc)
+
         part = rows_of(i, 256)
         total = None
         for jj in (0, 1):
@@ -772,6 +793,7 @@
             term = mm_nt(low, weight(1, jj, 0, 512))
             total = term if total is None else total + term
         send_part(0, i, total)
+        pl.when(jnp.logical_and(enc, i == 0))(lambda: memory_grad_pass(1))
 
     loop(2, ffn_back)
     for h in (0, 1):
@@ -784,7 +806,6 @@
         up_weights()
         for jj in (0, 1):
             reduce_first(1, jj, 0, enc)
-        reduce_pass(1, 1, enc)
 
     def ffn_back_after(part):
         d = r.DA[part] + ln_back(2, part, received(0, part))
@@ -802,27 +823,34 @@
         pl.when(dec)(lambda: heads_back(2, i))
 
     loop(2, after_ffn_back)
+    pl.when(enc)(lambda: reduce_pass(1, 1, enc))
 
     @pl.when(dec)
     def _():
-        attend_back(lambda jj: r.CQ[jj], r.CKV, 128, r.CKT, r.PX, 256, 0, 128)
-
-        def memory_back(i):
-            part = rows_of(i, 256)
-            pairs = jnp.concatenate([r.DQ[0, part, 0:256], r.DQ[1, part, 0:256]], axis=1)
-            r.DS[part] = mm_nt(pairs, both(2, 0, 256)).astype(BF)
-            for p in (0, 1):
-                memory_grad_swap(2 * i + p).start()
-
-        loop(2, memory_back)
+        attend_back(lambda jj: r.CQ[jj], r.CKV, 128, r.PX, 0, 128)
+
+        def memory_back(core):
+            groups = [pl.ds(pl.multiple_of(256 * i + 128 * core, 128), 128) for i in (0, 1)]
+            pairs = jnp.concatenate([
+                jnp.concatenate([r.DQ[0, part, 0:256], r.DQ[1, part, 0:256]], axis=1) for part in groups], axis=0)
+            grad = mm_nt(pairs, both(2, 0, 256))
+            r.DSF[groups[0]], r.DSF[groups[1]] = grad[0:128], grad[128:256]
+            grad = grad.astype(BF)
+            r.DS[groups[0]], r.DS[groups[1]] = grad[0:128], grad[128:256]
+
+        memory_back(sib)
+        for p in range(4):
+            memory_grad_swap(p).start()
+        memory_back(c)
 
         def memory_grad_out(i):
             part = half_rows(i, c)
             got(r.DSR.at[part], rs["dmx"].at[i])
-            r.DSO[part] = (r.DS[part].astype(F32) + r.DSR[part].astype(F32)).astype(BF)
+            r.DSO[part] = (r.DSF[part] + r.DSR[part].astype(F32)).astype(BF)
             memory_grad_copy(i).start()
 
         loop(4, memory_grad_out)
+        queries_back(r.CKT, 256)
         down_weights()
         for jj in (0, 1):
             reduce_first(1, jj, 1, dec)
@@ -857,12 +885,17 @@
 
     for jj in (0, 1):
         outer(0, jj, 384, 512, r.FB, lambda: r.HD[jj])
-    attend_back(lambda jj: r.QKV[jj, :, 0:128], r.QKV, 256, r.KT, r.PA, 0, 128, 256)
-
+    reduce_direct(0)
+    attend_back(lambda jj: r.QKV[jj, :, 0:128], r.QKV, 256, r.PA, 128, 256)
+
+    for jj in (0, 1):
+        outer(0, jj, 128, 384, r.N.at[0], lambda: r.DQ[jj, :, 128:384])
     reduce_pass(1, 0)
+    reduce_direct(1)
+    queries_back(r.KT, 0)
     for jj in (0, 1):
-        outer(0, jj, 0, 384, r.N.at[0], lambda: r.DQ[jj])
-        reduce_first(0, jj)
+        outer(0, jj, 0, 128, r.N.at[0], lambda: r.DQ[jj, :, 0:128])
+    reduce_direct(2)
 
     def first_back(i):
         part = rows_of(i, 256)
@@ -884,20 +917,20 @@
         quarter = 2 * c + h
         put_or_keep(lambda h=h, quarter=quarter: (r.DXB.at[rows_of(quarter, 128)], o_dx.at[m], ss["od"].at[h], rs["od"].at[m], role, quarter))
 
-    row_id = lax.broadcasted_iota(jnp.int32, (SMALL, T), 0)
-    halves = jnp.logical_and(row_id >= UPB, row_id < DOWNB)
-    r.SM2[...] = jnp.where(jnp.logical_or(halves, c == 0), r.SM[...], 0.0)
+    for row in range(6):
+        late = r.SM[DOWNB + row:DOWNB + row + 1] if row < 3 else jnp.zeros((1, T), F32)
+        r.SM2[row:row + 1] = jnp.where(c == 0, r.SM[row:row + 1], late)
+    for row in (0, 1):
+        r.SM2[6 + row:7 + row] = r.SM[pl.ds(UPB + 2 * c + row, 1), :]
     for d in (1, 2, 3):
         put(lambda d=d: (r.SM2, r.LM1.at[d - 1], ss["m1"].at[d - 1], rs["m1"].at[d - 1], dev(zz=zs[d])))
-    reduce_pass(0)
+    reduce_second(1)
     for d in range(3):
         got(r.LM1.at[d], rs["m1"].at[d])
     r.SM3[...] = r.SM2[...] + r.LM1[0] + r.LM1[1] + r.LM1[2]
     for d in (1, 2, 3):
         put(lambda d=d: (r.SM3, r.LM2.at[d - 1], ss["m2"].at[d - 1], rs["m2"].at[d - 1], dev(yy=ys[d])))
 
-    reduce_second(1)
-
     @pl.when(dec)
     def _():
         reduce_second(2)
@@ -905,24 +938,16 @@
     reduce_second(0)
     for d in range(3):
         got(r.LM2.at[d], rs["m2"].at[d])
-    r.SM[...] = r.SM3[...] + r.LM2[0] + r.LM2[1] + r.LM2[2]
+    r.SM4[...] = r.SM3[...] + r.LM2[0] + r.LM2[1] + r.LM2[2]
     for k in range(4):
-        put_or_keep(lambda k=k: (r.SM, o_sm.at[2 * m + c], ss["m3"].at[k], rs["m3"].at[2 * m + c], role, k))
+        put_or_keep(lambda k=k: (r.SM4, o_sm.at[2 * m + c], ss["m3"].at[k], rs["m3"].at[2 * m + c], role, k))
     reduce_third(1)
 
     @pl.when(dec)
     def _():
         reduce_third(2)
 
-    for k in range(4):
-        got(o_sm.at[k], rs["m3"].at[k])
-    for k in (0, 1):
-        got(o_st.at[k], rs["os"].at[k])
-        got(o_dx.at[k], rs["od"].at[k])
-        for g in (1, 2):
-            got(LC[g].at[k], rs["rc"].at[g, k])
-        for d in range(4):
-            got(o_c0.at[k, d], rs["r0"].at[k, d])
+    reduce_third(0)
 
     @pl.when(enc)
     def _():
@@ -939,15 +964,21 @@
 
     for end in ends:
         end()
+    for k in (0, 1):
+        got(o_st.at[k], rs["os"].at[k])
+        got(o_dx.at[k], rs["od"].at[k])
+    for k in range(4):
+        got(o_sm.at[k], rs["m3"].at[k])
+    for k in (0, 1):
+        for g in range(3):
+            got(LC[g].at[k], rs["rc"].at[g, k])
 
 
 def finish(st, dx, c0, c1, c2, small, o_st, o_dx, o_gain, o_shift, o_in, o_out, o_cross, o_up, o_upb, o_down, o_downb,
            o_haltw, o_haltb, o_act):
     o_st[...] = st[...]
     o_dx[...] = dx[...].astype(F32)
-    both = c0[0, 0].astype(F32)
-    for k in range(1, 8):
-        both = both + c0[k // 4, k % 4].astype(F32)
+    both = c0[0].astype(F32) + c0[1].astype(F32)
     for k in range(3):
         o_in[k] = both[:, 128 * k:128 * k + 128]
     o_out[...] = both[:, 384:512]
@@ -956,16 +987,17 @@
     both = c2[0].astype(F32) + c2[1].astype(F32)
     for k in (0, 1):
         o_cross[:, k, :] = both[:, 128 * k:128 * k + 128]
-    total = small[0] + small[1] + small[2] + small[3]
+    norms, rest = small[0] + small[2], small[1] + small[3]
     for k in range(3):
-        o_gain[k] = total[GAIN + k:GAIN + k + 1]
-        o_shift[k] = total[SHIFT + k:SHIFT + k + 1]
-    for k in range(4):
-        o_upb[:, 512 * k:512 * k + 512] = total[UPB + k:UPB + k + 1]
-    o_downb[...] = total[DOWNB:DOWNB + 1]
-    o_haltw[...] = total[HALTW:HALTW + 1]
-    o_haltb[...] = total[SCAL:SCAL + 1, 0:1]
-    ran, alive = total[SCAL:SCAL + 1, 1:2], total[SCAL:SCAL + 1, 2:3]
+        o_gain[k] = norms[GAIN + k:GAIN + k + 1]
+        o_shift[k] = norms[SHIFT + k:SHIFT + k + 1]
+    for k in (0, 1):
+        o_upb[:, 512 * k:512 * k + 512] = norms[6 + k:7 + k]
+        o_upb[:, 1024 + 512 * k:1536 + 512 * k] = rest[6 + k:7 + k]
+    o_downb[...] = rest[0:1]
+    o_haltw[...] = rest[1:2]
+    o_haltb[...] = rest[2:3, 0:1]
+    ran, alive = rest[2:3, 1:2], rest[2:3, 2:3]
     o_act[...] = jnp.concatenate([ran / alive, 1.0 - alive / (32 * T)], axis=1)
 
 
@@ -977,10 +1009,10 @@
         out_shape=[
             jax.ShapeDtypeStruct((2, 128, T), BF),
             jax.ShapeDtypeStruct((2, 128, T), BF),
-            jax.ShapeDtypeStruct((2, 4, 32, 512), BF),
+            jax.ShapeDtypeStruct((2, 32, 512), BF),
             jax.ShapeDtypeStruct((2, 32, 1024), BF),
             jax.ShapeDtypeStruct((2, 32, 256), BF),
-            jax.ShapeDtypeStruct((4, SMALL, T), F32),
+            jax.ShapeDtypeStruct((4, 8, T), F32),
         ],
         in_specs=[anywhere] * 2 + [vm] * 8 + [anywhere] * 2 + [vm] + [anywhere] * 2,
         out_specs=[anywhere] * 6,

time: 112 us -> 108 us (0.964)
  Pallas kernels: 109 us -> 106 us
    pallas_call x1, Pallas kernels: 107 us -> 104 us  [on_device(): pl.pallas_call(kernel, out_shape=[jax.ShapeDtypeStruct((2, 128, T), BF),...]
where the time goes in v3:
time: 108 us
  Pallas kernels  106 us (98%)
  between operations  1.48 us (1%)
    pallas_call x1, Pallas kernels, on_device(): pl.pallas_call(kernel, out_shape=[jax.ShapeDtypeStruct((2, 128, T), BF),...  104 us
    pallas_call x1, Pallas kernels, on_device(): pl.pallas_call(finish, out_shape=[jax.ShapeDtypeStruct((2, 128, T), BF),...  2.18 us

profile of v3, /device:TPU:0, one launch (start us, length us, event | category | flops | bytes accessed | tf_op | source)
XLA Modules:
  0.0 107.6 jit_solution(15432340709406124036)
XLA Ops:
  1.3 104.0 %step.1 = (bf16[2,128,512]{2,1,0:T(8,128)(2,1)}, bf16[2,128,512]{2,1,0:T(8,128)(2,1)}, bf16[2,32,512]{2,1,0:T(8,128)(2,1)}, bf16[2,32,1024]{2,1,0:T(8,128)(2,1)}...) custom-call(bf16[2,128,512]{2,1,0:T(8,128)(2,1)} %bitcast.35, bf16[2,128,512]{2,1,0:T(8,128)(2,1)} %bitcast.36, ...), custom_call_target="tpu_custom_call" | custom-call | tf_op jit(solution)/shard_map/step/pallas_call | solution.py:1007
  105.3 2.2 %finish.1 = (bf16[2,128,512]{2,1,0:T(8,128)(2,1)}, f32[2,128,512]{2,1,0:T(8,128)}, f32[3,1,512]{2,1,0:T(1,128)}, f32[3,1,512]{2,1,0:T(1,128)}, f32[3,32,128]{2,1...) custom-call(bf16[2,128,512]{2,1,0:T(8,128)(2,1)} %get-tuple-element., ...), custom_call_target="tpu_custom_call" | custom-call | tf_op jit(solution)/shard_map/finish/pallas_call | solution.py:1028

commit v4 on v3

--- a/solution.py
+++ b/solution.py
@@ -614,9 +614,8 @@
         r.KT[jj] = three[:, 128:256].T.astype(BF)
         r.VT[jj] = three[:, 256:384].T.astype(BF)
 
+    gather_pass(3)
     attend(lambda jj: r.QKV[jj, :, 0:128], r.QKV, 128, r.VT, r.BS, r.PA, r.HD)
-
-    gather_pass(3)
 
     @pl.when(dec)
     def _():

time: 108 us -> 107 us (level)
    pallas_call x1, Pallas kernels: 104 us -> 103 us  [on_device(): pl.pallas_call(kernel, out_shape=[jax.ShapeDtypeStruct((2, 128, T), BF),...]
where the time goes in v4:
time: 107 us; the launch traced here: 106 us
  Pallas kernels  105 us (98%)
  between operations  1.48 us (1%)
    pallas_call x1, Pallas kernels, on_device(): pl.pallas_call(kernel, out_shape=[jax.ShapeDtypeStruct((2, 128, T), BF),...  103 us
    pallas_call x1, Pallas kernels, on_device(): pl.pallas_call(finish, out_shape=[jax.ShapeDtypeStruct((2, 128, T), BF),...  2.18 us

profile of v4, /device:TPU:0, one launch (start us, length us, event | category | flops | bytes accessed | tf_op | source)
XLA Modules:
  0.0 106.5 jit_solution(10895525870449725654)
XLA Ops:
  1.3 102.8 %step.1 = (bf16[2,128,512]{2,1,0:T(8,128)(2,1)}, bf16[2,128,512]{2,1,0:T(8,128)(2,1)}, bf16[2,32,512]{2,1,0:T(8,128)(2,1)}, bf16[2,32,1024]{2,1,0:T(8,128)(2,1)}...) custom-call(bf16[2,128,512]{2,1,0:T(8,128)(2,1)} %bitcast.35, bf16[2,128,512]{2,1,0:T(8,128)(2,1)} %bitcast.36, ...), custom_call_target="tpu_custom_call" | custom-call | tf_op jit(solution)/shard_map/step/pallas_call | solution.py:1006
  104.1 2.2 %finish.1 = (bf16[2,128,512]{2,1,0:T(8,128)(2,1)}, f32[2,128,512]{2,1,0:T(8,128)}, f32[3,1,512]{2,1,0:T(1,128)}, f32[3,1,512]{2,1,0:T(1,128)}, f32[3,32,128]{2,1...) custom-call(bf16[2,128,512]{2,1,0:T(8,128)(2,1)} %get-tuple-element., ...), custom_call_target="tpu_custom_call" | custom-call | tf_op jit(solution)/shard_map/finish/pallas_call | solution.py:1027
